TPU v7x, 256 devices: a whole 4x4x8 slice. The times are simulated.
256 devices in a mesh: expert: 16 (over x, y_hi, core), tensor: 8 (over z), dp: 2 (over y_lo).
Axes of the slice: x: 4, y: 4 (y_hi: 2, y_lo: 2; y = y_hi * 2 + y_lo), z: 8, core: 2. Of those that a mesh axis runs over, the one named last changes fastest.
Arguments:
- tokens: bfloat16 [8192, 3072], P(('expert', 'dp'), 'tensor'), may hold values from -6 to 6
- out_grad: bfloat16 [8192, 3072], P(('expert', 'dp'), 'tensor'), may hold values from -6 to 6
- gate_weight: bfloat16 [5376, 3072], P('expert', 'tensor'), may hold values from -0.109375 to 0.109375
- up_weight: bfloat16 [5376, 3072], P('expert', 'tensor'), may hold values from -0.109375 to 0.109375
- down_weight: bfloat16 [5376, 3072], P('expert', 'tensor'), may hold values from -0.078125 to 0.078125
- route_count: int32 [32], P(('expert', 'dp')), may hold values from 24 to 96, as said below
- route_index: int32 [3072], P(('expert', 'dp')), may hold values from 0 to 255, as said below
- route_gate: float32 [3072], P(('expert', 'dp')), may hold values from 0.1 to 1
Outputs:
- mixed: bfloat16 [8192, 3072], P(('expert', 'dp'), 'tensor')
- input_grad: bfloat16 [8192, 3072], P(('expert', 'dp'), 'tensor')
- grad_gate: float32 [5376, 3072], P('expert', ('tensor', 'dp'))
- grad_up: float32 [5376, 3072], P('expert', ('tensor', 'dp'))
- grad_down: float32 [5376, 3072], P('expert', ('tensor', 'dp'))
Inputs may be any that keep to these rules, and one draw needn't show every extreme that they name: `route_count`: one shard's count is exactly 96 and another's exactly 24. `route_index`: within one shard's 96 slots the token indices are distinct.
All inputs are finite; a program needn't handle non-finite values.
Results may differ from a plain program's by a relative error of at most 0.035.
Values may be sent and summed in bfloat16 or wider, within the bound.
No kernel may reach another device: no remote copies, remote signals or barrier semaphores. Data moves between devices by JAX's collectives and lax.ppermute only.
A program may use at most 64 MiB of HBM per device.

v0:
```python
import functools

import jax
import jax.numpy as jnp
from jax import lax
from jax.experimental import pallas as pl
from jax.experimental.pallas import tpu as pltpu
from jax.sharding import Mesh
from jax.sharding import PartitionSpec as P

BF16 = jnp.bfloat16
F32 = jnp.float32
XS, YS, CORES, RING = 4, 2, 2, 8
CHIPS = XS * YS
FIRST, LAST = 640, 768
VMEM_LIMIT = 40 * 1024 * 1024
WHOLE = pl.BlockSpec(memory_space=pltpu.VMEM)
SCALARS = pl.BlockSpec(memory_space=pltpu.SMEM)


def dot(left, right, left_dim, right_dim):
    return lax.dot_general(
        left, right, (((left_dim,), (right_dim,)), ((), ())), preferred_element_type=F32
    )


def core_swap(x):
    return lax.ppermute(x, "core", [(0, 1), (1, 0)])


def among_chips(x):
    return lax.all_to_all(x, ("x", "y"), 0, 0, tiled=True)


def ring(x, by):
    return lax.ppermute(x, "tensor", [(z, (z + by) % RING) for z in range(RING)])


def local_call(body, name, out_shape, operands, scratch=()):
    return pl.pallas_call(
        body,
        out_shape=out_shape,
        in_specs=[SCALARS] + [WHOLE] * len(operands[1:]),
        out_specs=jax.tree.map(lambda _: WHOLE, out_shape),
        scratch_shapes=scratch,
        compiler_params=pltpu.CompilerParams(vmem_limit_bytes=VMEM_LIMIT),
        cost_estimate=pl.CostEstimate(flops=1, bytes_accessed=1, transcendentals=0),
        name=name,
    )(*operands)


def pre_body(deltas, where_ref, came_ref, other_ref, w_rows_ref, w_grads_ref, payload_ref, *refs):
    here, core = where_ref[0], where_ref[1]
    width = came_ref.shape[-1]
    w_rows, w_grads = w_rows_ref[...], w_grads_ref[...]
    for n, delta in enumerate(deltas):
        at = lax.rem(here + delta, RING)
        came, other = came_ref[at], other_ref[at]
        rows = jnp.where(core == 0, came, other)
        grads = jnp.where(core == 0, other, came)
        payload_ref[n, :, :width] = rows
        payload_ref[n, :, width:] = grads
        a, b = dot(rows, w_rows, 1, 1), dot(grads, w_grads, 1, 1)
        kind = refs[n].dtype
        refs[n][:, :FIRST] = a[:, :FIRST].astype(kind)
        refs[n][:, FIRST:LAST] = (a[:, FIRST:] + b[:, : LAST - FIRST]).astype(kind)
        refs[n][:, LAST:] = b[:, LAST - FIRST :].astype(kind)


def join(refs, to_ref):
    size = refs[0].shape[0]
    for n, ref in enumerate(refs):
        to_ref[n * size : (n + 1) * size, :] = ref[...]


def out_body(deltas, where_ref, w_rows_ref, w_grads_ref, *refs):
    core = where_ref[1]
    keep_ref, give_ref, acts_ref = refs[-3:]
    join(refs[:-3], acts_ref)
    size, width = refs[0].shape[0], w_rows_ref.shape[1]
    out = dot(acts_ref[:, FIRST:], w_grads_ref[...], 1, 0)
    back = dot(acts_ref[:, :LAST], w_rows_ref[...], 1, 0)
    for n in range(len(deltas)):
        for cols, part in ((slice(0, width), out), (slice(width, 2 * width), back)):
            low = part[2 * n * size : (2 * n + 1) * size]
            high = part[(2 * n + 1) * size : (2 * n + 2) * size]
            keep_ref[n, :, cols] = jnp.where(core == 0, low, high)
            give_ref[n, :, cols] = jnp.where(core == 0, high, low).astype(BF16)


def weight_body(block, where_ref, first_ref, rest_ref, *refs):
    dp = where_ref[2]
    keep_ref, give_ref, acts_ref = refs[-3:]
    join(refs[:-3], acts_ref)
    part = keep_ref.shape[0]
    split = first_ref.shape[0]
    width = 2 * part

    def product(cols, units):
        return dot(first_ref[:, cols], acts_ref[:split, units], 0, 0) + dot(
            rest_ref[:, cols], acts_ref[split:, units], 0, 0
        )

    by_rows = product(slice(0, width), slice(0, LAST))
    by_grads = product(slice(width, 2 * width), slice(FIRST, acts_ref.shape[1]))
    unit = FIRST + lax.broadcasted_iota(jnp.int32, (part, LAST - FIRST), 1)
    for cols in (slice(0, FIRST), slice(FIRST, LAST), slice(LAST, acts_ref.shape[1])):
        halves = []
        for rows in (slice(0, part), slice(part, width)):
            if cols.stop == FIRST:
                halves.append(by_rows[rows, :FIRST])
            elif cols.start == FIRST:
                halves.append(
                    jnp.where(
                        unit < 2 * block, by_rows[rows, FIRST:], by_grads[rows, : LAST - FIRST]
                    )
                )
            else:
                halves.append(by_grads[rows, LAST - FIRST :])
        keep_ref[:, cols] = jnp.where(dp == 0, halves[0], halves[1])
        give_ref[:, cols] = jnp.where(dp == 0, halves[1], halves[0]).astype(BF16)


def scatter_body(where_ref, came_ref, index_ref, weight_ref, live_ref, mixed_ref, grad_ref):
    total = came_ref[0].astype(F32)
    for n in range(1, CHIPS):
        total = total + came_ref[n].astype(F32)
    token_count, width = mixed_ref.shape
    out_rows = (weight_ref[...] * total[:, :width]).astype(BF16)
    back_rows = jnp.where(live_ref[...] > 0, total[:, width:], 0.0).astype(BF16)
    token = lax.broadcasted_iota(jnp.int32, (token_count, index_ref.shape[1]), 0)
    place = jnp.where(token == index_ref[...], 1.0, 0.0).astype(BF16)
    mixed_ref[...] = dot(place, out_rows, 1, 0).astype(BF16)
    grad_ref[...] = dot(place, back_rows, 1, 0).astype(BF16)


def sum_body(deltas, where_ref, keep_ref, got_ref, keep_last_ref, got_last_ref, out_ref):
    here = where_ref[0]
    for n, delta in enumerate(deltas):
        out_ref[lax.rem(here + delta, RING)] = (keep_ref[n] + got_ref[n].astype(F32)).astype(BF16)
    out_ref[lax.rem(here + RING // 2, RING)] = (
        keep_last_ref[0] + got_last_ref[0].astype(F32)
    ).astype(BF16)


def on_device(
    tokens, out_grad, gate_weight, up_weight, down_weight, route_count, route_index, route_gate
):
    capacity = route_index.shape[0]
    token_count, width = tokens.shape
    block = gate_weight.shape[0]
    units = 3 * block
    core = lax.axis_index("core")
    core0 = core == 0
    here = lax.axis_index("tensor")
    where = jnp.stack([here, core, lax.axis_index("dp")]).astype(jnp.int32)
    is_live = jnp.arange(capacity, dtype=jnp.int32) < route_count[0]
    route_weight = jnp.where(is_live, route_gate, 0.0)
    pick = (
        route_index[:, None] == jnp.arange(token_count, dtype=jnp.int32)[None, :]
    ).astype(BF16)
    rows_here = dot(pick, tokens, 1, 0).astype(BF16)
    grads_here = (route_weight[:, None] * dot(pick, out_grad, 1, 0)).astype(BF16)

    w_rows = jnp.concatenate(
        [gate_weight, up_weight, jnp.zeros((LAST - 2 * block, width), BF16)], axis=0
    )
    w_grads = jnp.concatenate(
        [jnp.zeros((2 * block - FIRST, width), BF16), down_weight], axis=0
    )

    mine = jnp.where(core0, rows_here, grads_here)
    got = core_swap(jnp.where(core0, grads_here, rows_here))
    piece = jnp.where(
        core0, jnp.concatenate([mine, got], axis=0), jnp.concatenate([got, mine], axis=0)
    )
    came = among_chips(jnp.broadcast_to(piece[None], (CHIPS,) + piece.shape))
    other = core_swap(came)
    pre = {}
    payloads = []
    first, rest = (4, 3, 5), (2, 6, 1, 7, 0)
    for deltas, name in ((first, "pre_first"), (rest, "pre_rest")):
        shapes = [jax.ShapeDtypeStruct((len(deltas), 2 * capacity, 2 * width), BF16)]
        for delta in deltas:
            shapes.append(
                jax.ShapeDtypeStruct((2 * capacity, units), BF16 if delta == 4 else F32)
            )
        payload, *blocks = local_call(
            functools.partial(pre_body, deltas), name, shapes, [where, came, other, w_rows, w_grads]
        )
        payloads.append(payload.reshape(-1, 2 * width))
        pre.update(zip(deltas, blocks))

    def half(delta, h):
        return pre[delta][h * capacity : (h + 1) * capacity]

    sums = []
    for h in range(2):
        left_path = (4, 5, 6, 7) if h == 0 else (5, 6, 7)
        right_path = (3, 2, 1) if h == 0 else (4, 3, 2, 1)
        ends = []
        for path, by in ((left_path, -1), (right_path, 1)):
            moving = None
            for delta in path:
                total = half(delta, h)
                if moving is not None:
                    total = total + moving.astype(F32)
                moving = ring(total.astype(BF16), by)
            ends.append(moving.astype(F32))
        sums.append(half(0, h) + ends[0] + ends[1])

    acts_own = []
    for total in sums:
        gate_pre, up_pre, d_hidden = (
            total[:, :block],
            total[:, block : 2 * block],
            total[:, 2 * block :],
        )
        sigmoid_gate = jax.nn.sigmoid(gate_pre)
        activated = gate_pre * sigmoid_gate
        hidden = (activated * up_pre).astype(BF16)
        d_gate = (
            d_hidden * up_pre * sigmoid_gate * (1.0 + gate_pre * (1.0 - sigmoid_gate))
        ).astype(BF16)
        d_up = (d_hidden * activated).astype(BF16)
        acts_own.append(jnp.concatenate([d_gate, d_up, hidden], axis=1))

    halves = {0: acts_own}
    right = list(acts_own)
    left = list(acts_own)
    for step in (1, 2, 3):
        right = [ring(a, 1) for a in right]
        left = [ring(a, -1) for a in left]
        halves[RING - step] = right
        halves[step] = left
    halves[4] = [ring(right[0], 1), ring(left[1], -1)]

    near, far = (0, 7, 1, 6, 2, 5, 3), (4,)
    kept, given = [], []
    for deltas, name in ((near, "out_near"), (far, "out_far")):
        shape = (len(deltas), capacity, 2 * width)
        pieces = [h for delta in deltas for h in halves[delta]]
        keep, give = local_call(
            functools.partial(out_body, deltas),
            name,
            [jax.ShapeDtypeStruct(shape, F32), jax.ShapeDtypeStruct(shape, BF16)],
            [where, w_rows, w_grads] + pieces,
            [pltpu.VMEM((len(pieces) * capacity, units), BF16)],
        )
        kept.append(keep)
        given.append(give)
    swapped = [core_swap(give) for give in lax.optimization_barrier(given)]

    part = width // 2
    pieces = [h for delta in first + rest for h in halves[delta]]
    keep_w, give_w = local_call(
        functools.partial(weight_body, block),
        "weight_grads",
        [jax.ShapeDtypeStruct((part, units), F32), jax.ShapeDtypeStruct((part, units), BF16)],
        [where] + payloads + pieces,
        [pltpu.VMEM((len(pieces) * capacity, units), BF16)],
    )
    swapped, give_w = lax.optimization_barrier((swapped, give_w))
    got_w = lax.ppermute(give_w, "dp", [(0, 1), (1, 0)])
    by_chip = local_call(
        functools.partial(sum_body, near),
        "pair_sum",
        jax.ShapeDtypeStruct((CHIPS, capacity, 2 * width), BF16),
        [where, kept[0], swapped[0], kept[1], swapped[1]],
    )
    arrived = among_chips(by_chip)
    mixed, input_grad = local_call(
        scatter_body,
        "scatter_rows",
        [jax.ShapeDtypeStruct((token_count, width), BF16)] * 2,
        [
            where,
            arrived,
            route_index[None, :],
            route_weight[:, None],
            is_live[:, None].astype(jnp.int32),
        ],
    )
    grads_w = keep_w + got_w.astype(F32)
    return (
        mixed,
        input_grad,
        grads_w[:, :block].T,
        grads_w[:, block : 2 * block].T,
        grads_w[:, 2 * block :].T,
    )


def solution(mesh):
    ways = (("x", "y", "core"), "tensor", "dp")
    chips = Mesh(mesh.devices.reshape(XS, YS, CORES, RING, 2), ways[0] + ways[1:])
    expert, tensor, dp = ways
    tokens = P(expert + (dp,), tensor)
    weight = P(expert, tensor)
    slots = P(expert + (dp,))
    grad = P(expert, (tensor, dp))
    return jax.shard_map(
        on_device,
        mesh=chips,
        in_specs=(tokens, tokens, weight, weight, weight, slots, slots, slots),
        out_specs=(tokens, tokens, grad, grad, grad),
        check_vma=False,
    )
```

profile of v0, /device:TPU:1, one launch (start us, length us, event | category | flops | bytes accessed | tf_op | source)
XLA Modules:
  0.0 150.9 jit_solution(3557763902312031407)
XLA Ops:
  4.1 3.3 %collective-permute-start = (bf16[96,384]{1,0:T(8,128)(2,1)S(1)}, bf16[96,384]{1,0:T(8,128)(2,1)S(1)}, u32[]{:S(2)}, u32[]{:S(2)}) collective-permute-start(bf16[96,384]{1,0:T(8,128)(2,1)S(1)} %get-tuple-element.73), channel_id=1, source_target_pairs={{0,16},{16,0},{1,17},{17,1},{2,18},{18,2},{3,19},{19,3},{4,20},{20... | collective-permute-start | bytes 221192 | tf_op jit(solution)/shard_map/ppermute | solution.py:28
  8.5 22.1 %all_to_all.10.came_ref = bf16[8,192,384]{2,1,0:T(8,128)(2,1)S(1)} all-to-all(bf16[8,192,384]{2,1,0:T(8,128)(2,1)S(1)} %broadcast_in_dim.26), channel_id=1, replica_groups=mesh['x'=4,'y'=2,'core'=2,'tensor'=8,'dp'=2] {'x','y'}, dimensions={0} | all-to-all | bytes 2359296 | tf_op jit(solution)/shard_map/all_to_all | solution.py:32
  30.6 2.1 %collective-permute-start.1 = (bf16[8,192,384]{2,1,0:T(8,128)(2,1)S(1)}, bf16[8,192,384]{2,1,0:T(8,128)(2,1)S(1)}, u32[]{:S(2)}, u32[]{:S(2)}) collective-permute-start(bf16[8,192,384]{2,1,0:T(8,128)(2,1)S(1)} %all_to_all.10.came_ref), channel_id=1, source_target_pairs={{0,16},{16,0},{1,17},{17,1},{2,18},{18,2},{3,19},{19,3},{4,20},{20... | collective-permute-start | bytes 3538952 | tf_op jit(solution)/shard_map/ppermute | solution.py:28
  40.4 2.4 %collective-permute-start.9 = (bf16[96,1008]{1,0:T(8,128)(2,1)S(1)}, bf16[96,1008]{1,0:T(8,128)(2,1)S(1)}, u32[]{:S(2)}, u32[]{:S(2)}) collective-permute-start(bf16[96,1008]{1,0:T(8,128)(2,1)S(1)} %slice.150), channel_id=1, source_target_pairs={{0,14},{2,0},{4,2},{6,4},{8,6},{10,8},{12,10},{14,12},{1,15},{3,1}... | collective-permute-start | bytes 580616 | tf_op jit(solution)/shard_map/ppermute | solution.py:36
  44.3 2.4 %pre_rest.1 = (bf16[5,192,768]{2,1,0:T(8,128)(2,1)S(1)}, f32[192,1008]{1,0:T(8,128)S(1)}, f32[192,1008]{1,0:T(8,128)S(1)}, f32[192,1008]{1,0:T(8,128)S(1)}, f32[...) custom-call(s32[3]{0:T(128)S(1)} %pad_add_fusion.where_ref, bf16[8,192,384]{2,1,0:T(8,128)(2,1)S(1)} %all_to_all.10.came_ref, ...), custom_call_target="tpu_custom_call" | custom-call | flops 1 | bytes 1 | tf_op jit(solution)/shard_map/pre_rest/pallas_call | solution.py:40
  47.7 3.3 %collective-permute-done.2 = bf16[96,1008]{1,0:T(8,128)(2,1)S(1)} collective-permute-done((bf16[96,1008]{1,0:T(8,128)(2,1)S(1)}, bf16[96,1008]{1,0:T(8,128)(2,1)S(1)}, u32[]{:S(2)}, u32[]{:S(2)}) %collective-permute-start.2) | collective-permute-done | bytes 193568 | tf_op jit(solution)/shard_map/ppermute | solution.py:36
  51.0 3.5 %collective-permute-start.3 = (bf16[96,1008]{1,0:T(8,128)(2,1)S(1)}, bf16[96,1008]{1,0:T(8,128)(2,1)S(1)}, u32[]{:S(2)}, u32[]{:S(2)}) collective-permute-start(bf16[96,1008]{1,0:T(8,128)(2,1)S(1)} %add_convert_fusion.9), channel_id=1, source_target_pairs={{0,14},{2,0},{4,2},{6,4},{8,6},{10,8},{12,10},{14,12},{1,15},{3,1}... | collective-permute-start | bytes 580616 | tf_op jit(solution)/shard_map/ppermute | solution.py:36
  57.6 3.5 %collective-permute-start.10 = (bf16[96,1008]{1,0:T(8,128)(2,1)S(1)}, bf16[96,1008]{1,0:T(8,128)(2,1)S(1)}, u32[]{:S(2)}, u32[]{:S(2)}) collective-permute-start(bf16[96,1008]{1,0:T(8,128)(2,1)S(1)} %get-tuple-element.58), channel_id=1, source_target_pairs={{0,14},{2,0},{4,2},{6,4},{8,6},{10,8},{12,10},{14,12},{1,15},{3,1}... | collective-permute-start | bytes 580616 | tf_op jit(solution)/shard_map/ppermute | solution.py:36
  61.3 4.3 %collective-permute-done.7 = bf16[96,1008]{1,0:T(8,128)(2,1)S(1)} collective-permute-done((bf16[96,1008]{1,0:T(8,128)(2,1)S(1)}, bf16[96,1008]{1,0:T(8,128)(2,1)S(1)}, u32[]{:S(2)}, u32[]{:S(2)}) %collective-permute-start.7) | collective-permute-done | bytes 193568 | tf_op jit(solution)/shard_map/ppermute | solution.py:36
  67.7 3.2 %collective-permute-start.11 = (bf16[96,1008]{1,0:T(8,128)(2,1)S(1)}, bf16[96,1008]{1,0:T(8,128)(2,1)S(1)}, u32[]{:S(2)}, u32[]{:S(2)}) collective-permute-start(bf16[96,1008]{1,0:T(8,128)(2,1)S(1)} %get-tuple-element.56), channel_id=1, source_target_pairs={{0,14},{2,0},{4,2},{6,4},{8,6},{10,8},{12,10},{14,12},{1,15},{3,1}... | collective-permute-start | bytes 580616 | tf_op jit(solution)/shard_map/ppermute | solution.py:36
  71.5 3.5 %collective-permute-done.8 = bf16[96,1008]{1,0:T(8,128)(2,1)S(1)} collective-permute-done((bf16[96,1008]{1,0:T(8,128)(2,1)S(1)}, bf16[96,1008]{1,0:T(8,128)(2,1)S(1)}, u32[]{:S(2)}, u32[]{:S(2)}) %collective-permute-start.8) | collective-permute-done | bytes 193568 | tf_op jit(solution)/shard_map/ppermute | solution.py:36
  75.0 2.7 %collective-permute-done.5 = bf16[96,1008]{1,0:T(8,128)(2,1)S(1)} collective-permute-done((bf16[96,1008]{1,0:T(8,128)(2,1)S(1)}, bf16[96,1008]{1,0:T(8,128)(2,1)S(1)}, u32[]{:S(2)}, u32[]{:S(2)}) %collective-permute-start.5) | collective-permute-done | bytes 193568 | tf_op jit(solution)/shard_map/ppermute | solution.py:36
  78.5 2.7 %collective-permute-start.19 = (bf16[96,1008]{1,0:T(8,128)(2,1)S(1)}, bf16[96,1008]{1,0:T(8,128)(2,1)S(1)}, u32[]{:S(2)}, u32[]{:S(2)}) collective-permute-start(bf16[96,1008]{1,0:T(8,128)(2,1)S(1)} %pad_maximum_fusion.1.refs_1_.refs_15_), channel_id=1, source_target_pairs={{0,14},{2,0},{4,2},{6,4},{8,6},{10,8},{12,10},{14,12},{1,15},{3,1}... | collective-permute-start | bytes 580616 | tf_op jit(solution)/shard_map/ppermute | solution.py:36
  84.1 2.9 %collective-permute-start.23 = (bf16[96,1008]{1,0:T(8,128)(2,1)S(1)}, bf16[96,1008]{1,0:T(8,128)(2,1)S(1)}, u32[]{:S(2)}, u32[]{:S(2)}) collective-permute-start(bf16[96,1008]{1,0:T(8,128)(2,1)S(1)} %collective-permute-done.19.refs_5_.refs_11_), channel_id=1, source_target_pairs={{0,14},{2,0},{4,2},{6,4},{8,6},{10,8},{12,10},{14,12},{1,15},{3,1}... | collective-permute-start | bytes 580616 | tf_op jit(solution)/shard_map/ppermute | solution.py:36
  89.8 3.0 %collective-permute-done.20.refs_6_.refs_8_ = bf16[96,1008]{1,0:T(8,128)(2,1)S(1)} collective-permute-done((bf16[96,1008]{1,0:T(8,128)(2,1)S(1)}, bf16[96,1008]{1,0:T(8,128)(2,1)S(1)}, u32[]{:S(2)}, u32[]{:S(2)}) %collective-permute-start.20) | collective-permute-done | bytes 193568 | tf_op jit(solution)/shard_map/ppermute | solution.py:36
  92.8 2.7 %collective-permute-start.27 = (bf16[96,1008]{1,0:T(8,128)(2,1)S(1)}, bf16[96,1008]{1,0:T(8,128)(2,1)S(1)}, u32[]{:S(2)}, u32[]{:S(2)}) collective-permute-start(bf16[96,1008]{1,0:T(8,128)(2,1)S(1)} %collective-permute-done.23.refs_9_.refs_7_), channel_id=1, source_target_pairs={{0,14},{2,0},{4,2},{6,4},{8,6},{10,8},{12,10},{14,12},{1,15},{3,1}... | collective-permute-start | bytes 580616 | tf_op jit(solution)/shard_map/ppermute | solution.py:36
  95.6 2.4 %collective-permute-start.26 = (bf16[96,1008]{1,0:T(8,128)(2,1)S(1)}, bf16[96,1008]{1,0:T(8,128)(2,1)S(1)}, u32[]{:S(2)}, u32[]{:S(2)}) collective-permute-start(bf16[96,1008]{1,0:T(8,128)(2,1)S(1)} %collective-permute-done.22.refs_8_.refs_6_), channel_id=1, source_target_pairs={{0,14},{2,0},{4,2},{6,4},{8,6},{10,8},{12,10},{14,12},{1,15},{3,1}... | collective-permute-start | bytes 580616 | tf_op jit(solution)/shard_map/ppermute | solution.py:36
  100.1 2.8 %collective-permute-start.29 = (bf16[96,1008]{1,0:T(8,128)(2,1)S(1)}, bf16[96,1008]{1,0:T(8,128)(2,1)S(1)}, u32[]{:S(2)}, u32[]{:S(2)}) collective-permute-start(bf16[96,1008]{1,0:T(8,128)(2,1)S(1)} %collective-permute-done.27.refs_13_.refs_3_), channel_id=1, source_target_pairs={{0,14},{2,0},{4,2},{6,4},{8,6},{10,8},{12,10},{14,12},{1,15},{3,1}... | collective-permute-start | bytes 580616 | tf_op jit(solution)/shard_map/ppermute | solution.py:36
  103.5 2.6 %collective-permute-done.25.refs_11_.refs_5_ = bf16[96,1008]{1,0:T(8,128)(2,1)S(1)} collective-permute-done((bf16[96,1008]{1,0:T(8,128)(2,1)S(1)}, bf16[96,1008]{1,0:T(8,128)(2,1)S(1)}, u32[]{:S(2)}, u32[]{:S(2)}) %collective-permute-start.25) | collective-permute-done | bytes 193568 | tf_op jit(solution)/shard_map/ppermute | solution.py:36
  106.1 2.4 %out_near.1 = (f32[7,96,768]{2,1,0:T(8,128)S(1)}, bf16[7,96,768]{2,1,0:T(8,128)(2,1)S(1)}) custom-call(s32[3]{0:T(128)S(1)} %pad_add_fusion.where_ref, bf16[768,384]{1,0:T(8,128)(2,1)S(1)} %maximum_maximum_fusion.w_rows_ref, bf16[368,384]{1,0:T(8,128)(2,1)S(1)} %concatenate.27.w_grads_ref, bf16[96,1008]{1,0:T(8,128)(2,1)S(1)} %pad_maximum_fusion.refs_0_.refs_14_, ...), custom_call_target="tpu_custom_call" | custom-call | flops 1 | bytes 1 | tf_op jit(solution)/shard_map/out_near/pallas_call | solution.py:40
  110.3 7.0 %collective-permute-start.30 = (bf16[7,96,768]{2,1,0:T(8,128)(2,1)S(1)}, bf16[7,96,768]{2,1,0:T(8,128)(2,1)S(1)}, u32[]{:S(2)}, u32[]{:S(2)}) collective-permute-start(bf16[7,96,768]{2,1,0:T(8,128)(2,1)S(1)} %get-tuple-element.39), channel_id=1, source_target_pairs={{0,16},{16,0},{1,17},{17,1},{2,18},{18,2},{3,19},{19,3},{4,20},{20... | collective-permute-start | bytes 3096584 | tf_op jit(solution)/shard_map/ppermute | solution.py:28
  117.4 2.6 %weight_grads.1 = (f32[192,1008]{1,0:T(8,128)S(1)}, bf16[192,1008]{1,0:T(8,128)(2,1)S(1)}) custom-call(s32[3]{0:T(128)S(1)} %pad_add_fusion.where_ref, bf16[576,768]{1,0:T(8,128)(2,1)S(1)} %bitcast.21, bf16[960,768]{1,0:T(8,128)(2,1)S(1)} %bitcast.20, bf16[96,1008]{1,0:T(8,128)(2,1)S(1)} %collective-permute-done.28.refs_0_, ...), custom_call_target="tpu_custom_call" | custom-call | flops 1 | bytes 1 | tf_op jit(solution)/shard_map/weight_grads/pallas_call | solution.py:40
  121.9 3.7 %all-to-all-start.1 = ((bf16[8,96,768]{2,1,0:T(8,128)(2,1)}), bf16[8,96,768]{2,1,0:T(8,128)(2,1)S(1)}, u32[]{:S(2)}, u32[]{:S(2)}) async-start(bf16[8,96,768]{2,1,0:T(8,128)(2,1)} %pair_sum.1), calls=%async_computation.1 | async-start | bytes 2359296 | tf_op jit(solution)/shard_map/all_to_all | solution.py:32
  126.2 21.8 %collective-permute-done.32 = bf16[192,1008]{1,0:T(8,128)(2,1)S(1)} collective-permute-done((bf16[192,1008]{1,0:T(8,128)(2,1)S(1)}, bf16[192,1008]{1,0:T(8,128)(2,1)S(1)}, u32[]{:S(2)}, u32[]{:S(2)}) %collective-permute-start.32) | collective-permute-done | bytes 387104 | tf_op jit(solution)/shard_map/ppermute | solution.py:264
  (92 shorter events, 36.3 us)
Async XLA Ops:
  37.0 10.6 %collective-permute-start.12 = (bf16[96,1008]{1,0:T(8,128)(2,1)S(1)}, bf16[96,1008]{1,0:T(8,128)(2,1)S(1)}, u32[]{:S(2)}, u32[]{:S(2)}) collective-permute-start(bf16[96,1008]{1,0:T(8,128)(2,1)S(1)} %get-tuple-element.67), channel_id=1, source_target_pairs={{0,2},{2,4},{4,6},{6,8},{8,10},{10,12},{12,14},{14,0},{1,3},{3,5},... | collective-permute-start | bytes 580616 | tf_op jit(solution)/shard_map/ppermute | solution.py:36
  38.7 15.8 %collective-permute-start.6 = (bf16[96,1008]{1,0:T(8,128)(2,1)S(1)}, bf16[96,1008]{1,0:T(8,128)(2,1)S(1)}, u32[]{:S(2)}, u32[]{:S(2)}) collective-permute-start(bf16[96,1008]{1,0:T(8,128)(2,1)S(1)} %slice.151), channel_id=1, source_target_pairs={{0,2},{2,4},{4,6},{6,8},{8,10},{10,12},{12,14},{14,0},{1,3},{3,5},... | collective-permute-start | bytes 580616 | tf_op jit(solution)/shard_map/ppermute | solution.py:36
  40.4 15.1 %collective-permute-start.9 = (bf16[96,1008]{1,0:T(8,128)(2,1)S(1)}, bf16[96,1008]{1,0:T(8,128)(2,1)S(1)}, u32[]{:S(2)}, u32[]{:S(2)}) collective-permute-start(bf16[96,1008]{1,0:T(8,128)(2,1)S(1)} %slice.150), channel_id=1, source_target_pairs={{0,14},{2,0},{4,2},{6,4},{8,6},{10,8},{12,10},{14,12},{1,15},{3,1}... | collective-permute-start | bytes 580616 | tf_op jit(solution)/shard_map/ppermute | solution.py:36
  42.8 8.1 %collective-permute-start.2 = (bf16[96,1008]{1,0:T(8,128)(2,1)S(1)}, bf16[96,1008]{1,0:T(8,128)(2,1)S(1)}, u32[]{:S(2)}, u32[]{:S(2)}) collective-permute-start(bf16[96,1008]{1,0:T(8,128)(2,1)S(1)} %get-tuple-element.68), channel_id=1, source_target_pairs={{0,14},{2,0},{4,2},{6,4},{8,6},{10,8},{12,10},{14,12},{1,15},{3,1}... | collective-permute-start | bytes 580616 | tf_op jit(solution)/shard_map/ppermute | solution.py:36
  47.6 7.6 %collective-permute-start.13 = (bf16[96,1008]{1,0:T(8,128)(2,1)S(1)}, bf16[96,1008]{1,0:T(8,128)(2,1)S(1)}, u32[]{:S(2)}, u32[]{:S(2)}) collective-permute-start(bf16[96,1008]{1,0:T(8,128)(2,1)S(1)} %add_convert_fusion.2), channel_id=1, source_target_pairs={{0,2},{2,4},{4,6},{6,8},{8,10},{10,12},{12,14},{14,0},{1,3},{3,5},... | collective-permute-start | bytes 580616 | tf_op jit(solution)/shard_map/ppermute | solution.py:36
  55.4 10.2 %collective-permute-start.7 = (bf16[96,1008]{1,0:T(8,128)(2,1)S(1)}, bf16[96,1008]{1,0:T(8,128)(2,1)S(1)}, u32[]{:S(2)}, u32[]{:S(2)}) collective-permute-start(bf16[96,1008]{1,0:T(8,128)(2,1)S(1)} %get-tuple-element.63), channel_id=1, source_target_pairs={{0,2},{2,4},{4,6},{6,8},{8,10},{10,12},{12,14},{14,0},{1,3},{3,5},... | collective-permute-start | bytes 580616 | tf_op jit(solution)/shard_map/ppermute | solution.py:36
  57.6 8.3 %collective-permute-start.10 = (bf16[96,1008]{1,0:T(8,128)(2,1)S(1)}, bf16[96,1008]{1,0:T(8,128)(2,1)S(1)}, u32[]{:S(2)}, u32[]{:S(2)}) collective-permute-start(bf16[96,1008]{1,0:T(8,128)(2,1)S(1)} %get-tuple-element.58), channel_id=1, source_target_pairs={{0,14},{2,0},{4,2},{6,4},{8,6},{10,8},{12,10},{14,12},{1,15},{3,1}... | collective-permute-start | bytes 580616 | tf_op jit(solution)/shard_map/ppermute | solution.py:36
  65.8 9.2 %collective-permute-start.8 = (bf16[96,1008]{1,0:T(8,128)(2,1)S(1)}, bf16[96,1008]{1,0:T(8,128)(2,1)S(1)}, u32[]{:S(2)}, u32[]{:S(2)}) collective-permute-start(bf16[96,1008]{1,0:T(8,128)(2,1)S(1)} %get-tuple-element.61), channel_id=1, source_target_pairs={{0,2},{2,4},{4,6},{6,8},{8,10},{10,12},{12,14},{14,0},{1,3},{3,5},... | collective-permute-start | bytes 580616 | tf_op jit(solution)/shard_map/ppermute | solution.py:36
  67.7 7.3 %collective-permute-start.11 = (bf16[96,1008]{1,0:T(8,128)(2,1)S(1)}, bf16[96,1008]{1,0:T(8,128)(2,1)S(1)}, u32[]{:S(2)}, u32[]{:S(2)}) collective-permute-start(bf16[96,1008]{1,0:T(8,128)(2,1)S(1)} %get-tuple-element.56), channel_id=1, source_target_pairs={{0,14},{2,0},{4,2},{6,4},{8,6},{10,8},{12,10},{14,12},{1,15},{3,1}... | collective-permute-start | bytes 580616 | tf_op jit(solution)/shard_map/ppermute | solution.py:36
  70.9 6.8 %collective-permute-start.5 = (bf16[96,1008]{1,0:T(8,128)(2,1)S(1)}, bf16[96,1008]{1,0:T(8,128)(2,1)S(1)}, u32[]{:S(2)}, u32[]{:S(2)}) collective-permute-start(bf16[96,1008]{1,0:T(8,128)(2,1)S(1)} %get-tuple-element.57), channel_id=1, source_target_pairs={{0,14},{2,0},{4,2},{6,4},{8,6},{10,8},{12,10},{14,12},{1,15},{3,1}... | collective-permute-start | bytes 580616 | tf_op jit(solution)/shard_map/ppermute | solution.py:36
  81.9 7.8 %collective-permute-start.17 = (bf16[96,1008]{1,0:T(8,128)(2,1)S(1)}, bf16[96,1008]{1,0:T(8,128)(2,1)S(1)}, u32[]{:S(2)}, u32[]{:S(2)}) collective-permute-start(bf16[96,1008]{1,0:T(8,128)(2,1)S(1)} %pad_maximum_fusion.1.refs_1_.refs_15_), channel_id=1, source_target_pairs={{0,2},{2,4},{4,6},{6,8},{8,10},{10,12},{12,14},{14,0},{1,3},{3,5},... | collective-permute-start | bytes 580616 | tf_op jit(solution)/shard_map/ppermute | solution.py:36
  84.1 8.7 %collective-permute-start.20 = (bf16[96,1008]{1,0:T(8,128)(2,1)S(1)}, bf16[96,1008]{1,0:T(8,128)(2,1)S(1)}, u32[]{:S(2)}, u32[]{:S(2)}) collective-permute-start(bf16[96,1008]{1,0:T(8,128)(2,1)S(1)} %collective-permute-done.16.refs_2_.refs_12_), channel_id=1, source_target_pairs={{0,2},{2,4},{4,6},{6,8},{8,10},{10,12},{12,14},{14,0},{1,3},{3,5},... | collective-permute-start | bytes 580616 | tf_op jit(solution)/shard_map/ppermute | solution.py:36
  84.1 8.7 %collective-permute-start.23 = (bf16[96,1008]{1,0:T(8,128)(2,1)S(1)}, bf16[96,1008]{1,0:T(8,128)(2,1)S(1)}, u32[]{:S(2)}, u32[]{:S(2)}) collective-permute-start(bf16[96,1008]{1,0:T(8,128)(2,1)S(1)} %collective-permute-done.19.refs_5_.refs_11_), channel_id=1, source_target_pairs={{0,14},{2,0},{4,2},{6,4},{8,6},{10,8},{12,10},{14,12},{1,15},{3,1}... | collective-permute-start | bytes 580616 | tf_op jit(solution)/shard_map/ppermute | solution.py:36
  87.7 7.9 %collective-permute-start.22 = (bf16[96,1008]{1,0:T(8,128)(2,1)S(1)}, bf16[96,1008]{1,0:T(8,128)(2,1)S(1)}, u32[]{:S(2)}, u32[]{:S(2)}) collective-permute-start(bf16[96,1008]{1,0:T(8,128)(2,1)S(1)} %collective-permute-done.18.refs_4_.refs_10_), channel_id=1, source_target_pairs={{0,14},{2,0},{4,2},{6,4},{8,6},{10,8},{12,10},{14,12},{1,15},{3,1}... | collective-permute-start | bytes 580616 | tf_op jit(solution)/shard_map/ppermute | solution.py:36
  89.8 8.2 %collective-permute-start.21 = (bf16[96,1008]{1,0:T(8,128)(2,1)S(1)}, bf16[96,1008]{1,0:T(8,128)(2,1)S(1)}, u32[]{:S(2)}, u32[]{:S(2)}) collective-permute-start(bf16[96,1008]{1,0:T(8,128)(2,1)S(1)} %collective-permute-done.17.refs_3_.refs_13_), channel_id=1, source_target_pairs={{0,2},{2,4},{4,6},{6,8},{8,10},{10,12},{12,14},{14,0},{1,3},{3,5},... | collective-permute-start | bytes 580616 | tf_op jit(solution)/shard_map/ppermute | solution.py:36
  92.8 7.3 %collective-permute-start.24 = (bf16[96,1008]{1,0:T(8,128)(2,1)S(1)}, bf16[96,1008]{1,0:T(8,128)(2,1)S(1)}, u32[]{:S(2)}, u32[]{:S(2)}) collective-permute-start(bf16[96,1008]{1,0:T(8,128)(2,1)S(1)} %collective-permute-done.20.refs_6_.refs_8_), channel_id=1, source_target_pairs={{0,2},{2,4},{4,6},{6,8},{8,10},{10,12},{12,14},{14,0},{1,3},{3,5},... | collective-permute-start | bytes 580616 | tf_op jit(solution)/shard_map/ppermute | solution.py:36
  92.8 7.3 %collective-permute-start.27 = (bf16[96,1008]{1,0:T(8,128)(2,1)S(1)}, bf16[96,1008]{1,0:T(8,128)(2,1)S(1)}, u32[]{:S(2)}, u32[]{:S(2)}) collective-permute-start(bf16[96,1008]{1,0:T(8,128)(2,1)S(1)} %collective-permute-done.23.refs_9_.refs_7_), channel_id=1, source_target_pairs={{0,14},{2,0},{4,2},{6,4},{8,6},{10,8},{12,10},{14,12},{1,15},{3,1}... | collective-permute-start | bytes 580616 | tf_op jit(solution)/shard_map/ppermute | solution.py:36
  95.6 7.9 %collective-permute-start.26 = (bf16[96,1008]{1,0:T(8,128)(2,1)S(1)}, bf16[96,1008]{1,0:T(8,128)(2,1)S(1)}, u32[]{:S(2)}, u32[]{:S(2)}) collective-permute-start(bf16[96,1008]{1,0:T(8,128)(2,1)S(1)} %collective-permute-done.22.refs_8_.refs_6_), channel_id=1, source_target_pairs={{0,14},{2,0},{4,2},{6,4},{8,6},{10,8},{12,10},{14,12},{1,15},{3,1}... | collective-permute-start | bytes 580616 | tf_op jit(solution)/shard_map/ppermute | solution.py:36
  98.0 8.1 %collective-permute-start.25 = (bf16[96,1008]{1,0:T(8,128)(2,1)S(1)}, bf16[96,1008]{1,0:T(8,128)(2,1)S(1)}, u32[]{:S(2)}, u32[]{:S(2)}) collective-permute-start(bf16[96,1008]{1,0:T(8,128)(2,1)S(1)} %collective-permute-done.21.refs_7_.refs_9_), channel_id=1, source_target_pairs={{0,2},{2,4},{4,6},{6,8},{8,10},{10,12},{12,14},{14,0},{1,3},{3,5},... | collective-permute-start | bytes 580616 | tf_op jit(solution)/shard_map/ppermute | solution.py:36
  100.1 9.2 %collective-permute-start.28 = (bf16[96,1008]{1,0:T(8,128)(2,1)S(1)}, bf16[96,1008]{1,0:T(8,128)(2,1)S(1)}, u32[]{:S(2)}, u32[]{:S(2)}) collective-permute-start(bf16[96,1008]{1,0:T(8,128)(2,1)S(1)} %collective-permute-done.24.refs_10_.refs_4_), channel_id=1, source_target_pairs={{0,2},{2,4},{4,6},{6,8},{8,10},{10,12},{12,14},{14,0},{1,3},{3,5},... | collective-permute-start | bytes 580616 | tf_op jit(solution)/shard_map/ppermute | solution.py:36
  100.1 9.2 %collective-permute-start.29 = (bf16[96,1008]{1,0:T(8,128)(2,1)S(1)}, bf16[96,1008]{1,0:T(8,128)(2,1)S(1)}, u32[]{:S(2)}, u32[]{:S(2)}) collective-permute-start(bf16[96,1008]{1,0:T(8,128)(2,1)S(1)} %collective-permute-done.27.refs_13_.refs_3_), channel_id=1, source_target_pairs={{0,14},{2,0},{4,2},{6,4},{8,6},{10,8},{12,10},{14,12},{1,15},{3,1}... | collective-permute-start | bytes 580616 | tf_op jit(solution)/shard_map/ppermute | solution.py:36
  110.3 9.7 %collective-permute-start.30 = (bf16[7,96,768]{2,1,0:T(8,128)(2,1)S(1)}, bf16[7,96,768]{2,1,0:T(8,128)(2,1)S(1)}, u32[]{:S(2)}, u32[]{:S(2)}) collective-permute-start(bf16[7,96,768]{2,1,0:T(8,128)(2,1)S(1)} %get-tuple-element.39), channel_id=1, source_target_pairs={{0,16},{16,0},{1,17},{17,1},{2,18},{18,2},{3,19},{19,3},{4,20},{20... | collective-permute-start | bytes 3096584 | tf_op jit(solution)/shard_map/ppermute | solution.py:28
  121.9 27.3 %all-to-all-start.1 = ((bf16[8,96,768]{2,1,0:T(8,128)(2,1)}), bf16[8,96,768]{2,1,0:T(8,128)(2,1)S(1)}, u32[]{:S(2)}, u32[]{:S(2)}) async-start(bf16[8,96,768]{2,1,0:T(8,128)(2,1)} %pair_sum.1), calls=%async_computation.1 | async-start | bytes 2359296 | tf_op jit(solution)/shard_map/all_to_all | solution.py:32
  125.6 22.4 %collective-permute-start.32 = (bf16[192,1008]{1,0:T(8,128)(2,1)S(1)}, bf16[192,1008]{1,0:T(8,128)(2,1)S(1)}, u32[]{:S(2)}, u32[]{:S(2)}) collective-permute-start(bf16[192,1008]{1,0:T(8,128)(2,1)S(1)} %get-tuple-element.50), channel_id=1, source_target_pairs={{0,1},{1,0},{2,3},{3,2},{4,5},{5,4},{6,7},{7,6},{8,9},{9,8},{10,11... | collective-permute-start | bytes 1161224 | tf_op jit(solution)/shard_map/ppermute | solution.py:264
  (16 other events, 135.3 us)
where the time goes:
time: 151 us
  waiting for transfers between devices  55.7 us (37%)
  starting transfers between devices  52.2 us (35%)
  blocking collectives  22.1 us (15%)
  Pallas kernels  13.6 us (9%)
  other arithmetic  2.08 us (1%)
  matrix products  2.03 us (1%)
  between operations  1.67 us (1%)
  local copies, waits for them, and re-layouts  1.54 us (1%)
    ppermute x28, starting transfers between devices, ring(): lax.ppermute(x, 'tensor', [(z, (z + by) % RING) for z in range(RING)])  35.4 us
    ppermute x28, waiting for transfers between devices, ring(): lax.ppermute(x, 'tensor', [(z, (z + by) % RING) for z in range(RING)])  30.9 us
    all_to_all x1, blocking collectives, among_chips(): return lax.all_to_all(x, ('x', 'y'), 0, 0, tiled=True)  22.1 us
    ppermute x1, waiting for transfers between devices, on_device(): got_w = lax.ppermute(give_w, 'dp', [(0, 1), (1, 0)])  21.8 us
    pallas_call x7, Pallas kernels, local_call(): pl.pallas_call(body, out_shape=out_shape, in_specs=[SCALARS] + [WHOLE] *...  13.6 us
    ppermute x4, starting transfers between devices, core_swap(): return lax.ppermute(x, 'core', [(0, 1), (1, 0)])  12.6 us
    all_to_all x1, starting transfers between devices, among_chips(): return lax.all_to_all(x, ('x', 'y'), 0, 0, tiled=True)  3.69 us
  transfers between devices with their start and end apart: 34, of which 20 were waited for; matrix products, arithmetic and copies ran while one was open for 2% of the time, Pallas kernels for 5%

commit v1 on v0

--- a/solution.py
+++ b/solution.py
@@ -51,20 +51,20 @@
 
 def pre_body(deltas, where_ref, came_ref, other_ref, w_rows_ref, w_grads_ref, payload_ref, *refs):
     here, core = where_ref[0], where_ref[1]
-    width = came_ref.shape[-1]
-    w_rows, w_grads = w_rows_ref[...], w_grads_ref[...]
+    size, width = came_ref.shape[1:]
     for n, delta in enumerate(deltas):
         at = lax.rem(here + delta, RING)
         came, other = came_ref[at], other_ref[at]
-        rows = jnp.where(core == 0, came, other)
-        grads = jnp.where(core == 0, other, came)
-        payload_ref[n, :, :width] = rows
-        payload_ref[n, :, width:] = grads
-        a, b = dot(rows, w_rows, 1, 1), dot(grads, w_grads, 1, 1)
-        kind = refs[n].dtype
-        refs[n][:, :FIRST] = a[:, :FIRST].astype(kind)
-        refs[n][:, FIRST:LAST] = (a[:, FIRST:] + b[:, : LAST - FIRST]).astype(kind)
-        refs[n][:, LAST:] = b[:, LAST - FIRST :].astype(kind)
+        payload_ref[n * size : (n + 1) * size, :width] = jnp.where(core == 0, came, other)
+        payload_ref[n * size : (n + 1) * size, width:] = jnp.where(core == 0, other, came)
+    by_rows = dot(payload_ref[:, :width], w_rows_ref[...], 1, 1)
+    by_grads = dot(payload_ref[:, width:], w_grads_ref[...], 1, 1)
+    mixed = by_rows[:, FIRST:] + by_grads[:, : LAST - FIRST]
+    for n, ref in enumerate(refs):
+        rows, kind = slice(n * size, (n + 1) * size), ref.dtype
+        ref[:, :FIRST] = by_rows[rows, :FIRST].astype(kind)
+        ref[:, FIRST:LAST] = mixed[rows].astype(kind)
+        ref[:, LAST:] = by_grads[rows, LAST - FIRST :].astype(kind)
 
 
 def join(refs, to_ref):
@@ -73,33 +73,30 @@
         to_ref[n * size : (n + 1) * size, :] = ref[...]
 
 
-def out_body(deltas, where_ref, w_rows_ref, w_grads_ref, *refs):
+def out_body(where_ref, w_rows_ref, w_grads_ref, *refs):
     core = where_ref[1]
     keep_ref, give_ref, acts_ref = refs[-3:]
     join(refs[:-3], acts_ref)
-    size, width = refs[0].shape[0], w_rows_ref.shape[1]
     out = dot(acts_ref[:, FIRST:], w_grads_ref[...], 1, 0)
     back = dot(acts_ref[:, :LAST], w_rows_ref[...], 1, 0)
-    for n in range(len(deltas)):
-        for cols, part in ((slice(0, width), out), (slice(width, 2 * width), back)):
-            low = part[2 * n * size : (2 * n + 1) * size]
-            high = part[(2 * n + 1) * size : (2 * n + 2) * size]
-            keep_ref[n, :, cols] = jnp.where(core == 0, low, high)
-            give_ref[n, :, cols] = jnp.where(core == 0, high, low).astype(BF16)
-
-
-def weight_body(block, where_ref, first_ref, rest_ref, *refs):
+    keep_ref[...] = jnp.where(core == 0, out, back)
+    give_ref[...] = jnp.where(core == 0, back, out).astype(BF16)
+
+
+def weight_body(block, where_ref, *refs):
     dp = where_ref[2]
-    keep_ref, give_ref, acts_ref = refs[-3:]
-    join(refs[:-3], acts_ref)
+    payload_refs = refs[:4]
+    keep_ref, give_ref, acts_ref, payload_ref = refs[-4:]
+    join(refs[4:-4], acts_ref)
+    at = 0
+    for ref in payload_refs:
+        payload_ref[at : at + ref.shape[0], :] = ref[...]
+        at += ref.shape[0]
     part = keep_ref.shape[0]
-    split = first_ref.shape[0]
     width = 2 * part
 
     def product(cols, units):
-        return dot(first_ref[:, cols], acts_ref[:split, units], 0, 0) + dot(
-            rest_ref[:, cols], acts_ref[split:, units], 0, 0
-        )
+        return dot(payload_ref[:, cols], acts_ref[:, units], 0, 0)
 
     by_rows = product(slice(0, width), slice(0, LAST))
     by_grads = product(slice(width, 2 * width), slice(FIRST, acts_ref.shape[1]))
@@ -134,13 +131,40 @@
     grad_ref[...] = dot(place, back_rows, 1, 0).astype(BF16)
 
 
-def sum_body(deltas, where_ref, keep_ref, got_ref, keep_last_ref, got_last_ref, out_ref):
+def pair_body(deltas, where_ref, keep_ref, got_ref, keep_last_ref, got_last_ref, out_ref):
     here = where_ref[0]
+    size = out_ref.shape[1]
     for n, delta in enumerate(deltas):
-        out_ref[lax.rem(here + delta, RING)] = (keep_ref[n] + got_ref[n].astype(F32)).astype(BF16)
+        rows = slice(n * size, (n + 1) * size)
+        out_ref[lax.rem(here + delta, RING)] = (
+            keep_ref[rows] + got_ref[rows].astype(F32)
+        ).astype(BF16)
     out_ref[lax.rem(here + RING // 2, RING)] = (
-        keep_last_ref[0] + got_last_ref[0].astype(F32)
+        keep_last_ref[...] + got_last_ref[...].astype(F32)
     ).astype(BF16)
+
+
+def chip_body(where_ref, a_ref, b_ref, own_ref, give_ref):
+    core = where_ref[1]
+    totals = []
+    for ref in (a_ref, b_ref):
+        total = ref[0].astype(F32)
+        for n in range(1, CHIPS):
+            total = total + ref[n].astype(F32)
+        totals.append(total)
+    own_ref[...] = jnp.where(core == 0, totals[0], totals[1])
+    give_ref[...] = jnp.where(core == 0, totals[1], totals[0]).astype(BF16)
+
+
+def scatter_body(where_ref, own_ref, got_ref, index_ref, weight_ref, live_ref, mixed_ref, grad_ref):
+    core = where_ref[1]
+    own, got = own_ref[...], got_ref[...].astype(F32)
+    out_rows = (weight_ref[...] * jnp.where(core == 0, own, got)).astype(BF16)
+    back_rows = jnp.where(live_ref[...] > 0, jnp.where(core == 0, got, own), 0.0).astype(BF16)
+    token = lax.broadcasted_iota(jnp.int32, (mixed_ref.shape[0], index_ref.shape[1]), 0)
+    place = jnp.where(token == index_ref[...], 1.0, 0.0).astype(BF16)
+    mixed_ref[...] = dot(place, out_rows, 1, 0).astype(BF16)
+    grad_ref[...] = dot(place, back_rows, 1, 0).astype(BF16)
 
 
 def on_device(
@@ -171,28 +195,26 @@
 
     mine = jnp.where(core0, rows_here, grads_here)
     got = core_swap(jnp.where(core0, grads_here, rows_here))
-    piece = jnp.where(
-        core0, jnp.concatenate([mine, got], axis=0), jnp.concatenate([got, mine], axis=0)
-    )
-    came = among_chips(jnp.broadcast_to(piece[None], (CHIPS,) + piece.shape))
-    other = core_swap(came)
+    chunks = (jnp.where(core0, mine, got), jnp.where(core0, got, mine))
     pre = {}
     payloads = []
     first, rest = (4, 3, 5), (2, 6, 1, 7, 0)
-    for deltas, name in ((first, "pre_first"), (rest, "pre_rest")):
-        shapes = [jax.ShapeDtypeStruct((len(deltas), 2 * capacity, 2 * width), BF16)]
-        for delta in deltas:
-            shapes.append(
-                jax.ShapeDtypeStruct((2 * capacity, units), BF16 if delta == 4 else F32)
+    for h, piece in enumerate(chunks):
+        came = among_chips(jnp.broadcast_to(piece[None], (CHIPS,) + piece.shape))
+        other = core_swap(came)
+        for deltas, name in ((first, "pre_first"), (rest, "pre_rest")):
+            shapes = [jax.ShapeDtypeStruct((len(deltas) * capacity, 2 * width), BF16)]
+            for delta in deltas:
+                starts = delta == 4 or (delta, h) in ((3, 0), (5, 1))
+                shapes.append(jax.ShapeDtypeStruct((capacity, units), BF16 if starts else F32))
+            payload, *blocks = local_call(
+                functools.partial(pre_body, deltas),
+                name,
+                shapes,
+                [where, came, other, w_rows, w_grads],
             )
-        payload, *blocks = local_call(
-            functools.partial(pre_body, deltas), name, shapes, [where, came, other, w_rows, w_grads]
-        )
-        payloads.append(payload.reshape(-1, 2 * width))
-        pre.update(zip(deltas, blocks))
-
-    def half(delta, h):
-        return pre[delta][h * capacity : (h + 1) * capacity]
+            payloads.append(payload)
+            pre.update({(delta, h): part for delta, part in zip(deltas, blocks)})
 
     sums = []
     for h in range(2):
@@ -202,12 +224,12 @@
         for path, by in ((left_path, -1), (right_path, 1)):
             moving = None
             for delta in path:
-                total = half(delta, h)
+                total = pre[delta, h]
                 if moving is not None:
                     total = total + moving.astype(F32)
                 moving = ring(total.astype(BF16), by)
             ends.append(moving.astype(F32))
-        sums.append(half(0, h) + ends[0] + ends[1])
+        sums.append(pre[0, h] + ends[0] + ends[1])
 
     acts_own = []
     for total in sums:
@@ -235,47 +257,62 @@
         halves[step] = left
     halves[4] = [ring(right[0], 1), ring(left[1], -1)]
 
-    near, far = (0, 7, 1, 6, 2, 5, 3), (4,)
+    near = (0, 7, 1, 6, 2, 5, 3)
     kept, given = [], []
-    for deltas, name in ((near, "out_near"), (far, "out_far")):
-        shape = (len(deltas), capacity, 2 * width)
-        pieces = [h for delta in deltas for h in halves[delta]]
-        keep, give = local_call(
-            functools.partial(out_body, deltas),
-            name,
-            [jax.ShapeDtypeStruct(shape, F32), jax.ShapeDtypeStruct(shape, BF16)],
-            [where, w_rows, w_grads] + pieces,
-            [pltpu.VMEM((len(pieces) * capacity, units), BF16)],
+    for h in range(2):
+        for deltas, name in ((near, "out_near"), ((4,), "out_far")):
+            shape = (len(deltas) * capacity, width)
+            keep, give = local_call(
+                out_body,
+                name,
+                [jax.ShapeDtypeStruct(shape, F32), jax.ShapeDtypeStruct(shape, BF16)],
+                [where, w_rows, w_grads] + [halves[delta][h] for delta in deltas],
+                [pltpu.VMEM((len(deltas) * capacity, units), BF16)],
+            )
+            kept.append(keep)
+            given.append(give)
+    arrived = []
+    for h in range(2):
+        swapped = [core_swap(g) for g in lax.optimization_barrier(given[2 * h : 2 * h + 2])]
+        by_chip = local_call(
+            functools.partial(pair_body, near),
+            "pair_sum",
+            jax.ShapeDtypeStruct((CHIPS, capacity, width), BF16),
+            [where, kept[2 * h], swapped[0], kept[2 * h + 1], swapped[1]],
         )
-        kept.append(keep)
-        given.append(give)
-    swapped = [core_swap(give) for give in lax.optimization_barrier(given)]
+        arrived.append(among_chips(by_chip))
 
     part = width // 2
-    pieces = [h for delta in first + rest for h in halves[delta]]
+    pieces = [halves[delta][h] for h in range(2) for delta in first + rest]
     keep_w, give_w = local_call(
         functools.partial(weight_body, block),
         "weight_grads",
         [jax.ShapeDtypeStruct((part, units), F32), jax.ShapeDtypeStruct((part, units), BF16)],
         [where] + payloads + pieces,
-        [pltpu.VMEM((len(pieces) * capacity, units), BF16)],
-    )
-    swapped, give_w = lax.optimization_barrier((swapped, give_w))
+        [
+            pltpu.VMEM((len(pieces) * capacity, units), BF16),
+            pltpu.VMEM((len(pieces) * capacity, 2 * width), BF16),
+        ],
+    )
     got_w = lax.ppermute(give_w, "dp", [(0, 1), (1, 0)])
-    by_chip = local_call(
-        functools.partial(sum_body, near),
-        "pair_sum",
-        jax.ShapeDtypeStruct((CHIPS, capacity, 2 * width), BF16),
-        [where, kept[0], swapped[0], kept[1], swapped[1]],
-    )
-    arrived = among_chips(by_chip)
+
+    own, give = local_call(
+        chip_body,
+        "chip_sum",
+        [
+            jax.ShapeDtypeStruct((capacity, width), F32),
+            jax.ShapeDtypeStruct((capacity, width), BF16),
+        ],
+        [where] + arrived,
+    )
     mixed, input_grad = local_call(
         scatter_body,
         "scatter_rows",
         [jax.ShapeDtypeStruct((token_count, width), BF16)] * 2,
         [
             where,
-            arrived,
+            own,
+            core_swap(give),
             route_index[None, :],
             route_weight[:, None],
             is_live[:, None].astype(jnp.int32),

time: 151 us -> 181 us (1.20)
  starting transfers between devices: 52.2 us -> 76.1 us
  local copies, waits for them, and re-layouts: 1.54 us -> 15.7 us
  waiting for transfers between devices: 55.7 us -> 46.2 us
  blocking collectives: 22.1 us -> 16.1 us
  Pallas kernels: 13.6 us -> 19.4 us
    ppermute x1, waiting for transfers between devices: 21.8 us -> 1 us  [on_device(): got_w = lax.ppermute(give_w, 'dp', [(0, 1), (1, 0)])]
    all_to_all x1 -> x3, waiting for transfers between devices: 0.01 us -> 16 us  [among_chips(): return lax.all_to_all(x, ('x', 'y'), 0, 0, tiled=True)]
    unnamed x12 -> x66, local copies, waits for them, and re-layouts: 0.04 us -> 13.4 us
    ppermute x4 -> x8, starting transfers between devices: 12.6 us -> 25.8 us  [core_swap(): return lax.ppermute(x, 'core', [(0, 1), (1, 0)])]
    all_to_all x1 -> x3, starting transfers between devices: 3.69 us -> 14.7 us  [among_chips(): return lax.all_to_all(x, ('x', 'y'), 0, 0, tiled=True)]
    all_to_all x1, blocking collectives: 22.1 us -> 16.1 us  [among_chips(): return lax.all_to_all(x, ('x', 'y'), 0, 0, tiled=True)]
    pallas_call x7 -> x13, Pallas kernels: 13.6 us -> 19.4 us  [local_call(): pl.pallas_call(body, out_shape=out_shape, in_specs=[SCALARS] + [WHOLE] *...]
    ppermute x28, waiting for transfers between devices: 30.9 us -> 28.3 us  [ring(): lax.ppermute(x, 'tensor', [(z, (z + by) % RING) for z in range(RING)])]
  transfers between devices with their start and end apart: 34 -> 40, of which waited for: 20 -> 17; matrix products, arithmetic and copies ran while one was open for 2% -> 2% of each run, Pallas kernels for 5% -> 9%
where the time goes in v1:
time: 181 us
  starting transfers between devices  76.1 us (42%)
  waiting for transfers between devices  46.2 us (26%)
  Pallas kernels  19.4 us (11%)
  blocking collectives  16.1 us (9%)
  local copies, waits for them, and re-layouts  15.7 us (9%)
  other arithmetic  3.19 us (2%)
  matrix products  2.03 us (1%)
  between operations  1.9 us (1%)
    ppermute x28, starting transfers between devices, ring(): lax.ppermute(x, 'tensor', [(z, (z + by) % RING) for z in range(RING)])  35.2 us
    ppermute x28, waiting for transfers between devices, ring(): lax.ppermute(x, 'tensor', [(z, (z + by) % RING) for z in range(RING)])  28.3 us
    ppermute x8, starting transfers between devices, core_swap(): return lax.ppermute(x, 'core', [(0, 1), (1, 0)])  25.8 us
    pallas_call x13, Pallas kernels, local_call(): pl.pallas_call(body, out_shape=out_shape, in_specs=[SCALARS] + [WHOLE] *...  19.4 us
    all_to_all x1, blocking collectives, among_chips(): return lax.all_to_all(x, ('x', 'y'), 0, 0, tiled=True)  16.1 us
    all_to_all x3, waiting for transfers between devices, among_chips(): return lax.all_to_all(x, ('x', 'y'), 0, 0, tiled=True)  16 us
    all_to_all x3, starting transfers between devices, among_chips(): return lax.all_to_all(x, ('x', 'y'), 0, 0, tiled=True)  14.7 us
    unnamed x66, local copies, waits for them, and re-layouts  13.4 us
  transfers between devices with their start and end apart: 40, of which 17 were waited for; matrix products, arithmetic and copies ran while one was open for 2% of the time, Pallas kernels for 9%

profile of v1, /device:TPU:1, one launch (start us, length us, event | category | flops | bytes accessed | tf_op | source)
XLA Modules:
  0.0 180.5 jit_solution(6523895480995855265)
XLA Ops:
  4.1 3.3 %collective-permute-start = (bf16[96,384]{1,0:T(8,128)(2,1)S(1)}, bf16[96,384]{1,0:T(8,128)(2,1)S(1)}, u32[]{:S(2)}, u32[]{:S(2)}) collective-permute-start(bf16[96,384]{1,0:T(8,128)(2,1)S(1)} %get-tuple-element.92), channel_id=1, source_target_pairs={{0,16},{16,0},{1,17},{17,1},{2,18},{18,2},{3,19},{19,3},{4,20},{20... | collective-permute-start | bytes 221192 | tf_op jit(solution)/shard_map/ppermute | solution.py:28
  8.4 16.1 %all_to_all.20.came_ref = bf16[8,96,384]{2,1,0:T(8,128)(2,1)S(1)} all-to-all(bf16[8,96,384]{2,1,0:T(8,128)(2,1)S(1)} %broadcast_in_dim.17), channel_id=1, replica_groups=mesh['x'=4,'y'=2,'core'=2,'tensor'=8,'dp'=2] {'x','y'}, dimensions={0} | all-to-all | bytes 1179648 | tf_op jit(solution)/shard_map/all_to_all | solution.py:32
  25.4 3.7 %all-to-all-start = ((bf16[8,96,384]{2,1,0:T(8,128)(2,1)}), bf16[8,96,384]{2,1,0:T(8,128)(2,1)S(1)}, u32[]{:S(2)}, u32[]{:S(2)}) async-start(bf16[8,96,384]{2,1,0:T(8,128)(2,1)} %broadcast_in_dim.16), calls=%async_computation | async-start | bytes 1179648 | tf_op jit(solution)/shard_map/all_to_all | solution.py:32
  31.0 7.0 %all-to-all-done.came_ref = bf16[8,96,384]{2,1,0:T(8,128)(2,1)S(1)} async-done(((bf16[8,96,384]{2,1,0:T(8,128)(2,1)}), bf16[8,96,384]{2,1,0:T(8,128)(2,1)S(1)}, u32[]{:S(2)}, u32[]{:S(2)}) %all-to-all-start) | async-done | bytes 589856 | tf_op jit(solution)/shard_map/all_to_all | solution.py:32
  38.0 3.6 %collective-permute-start.1 = (bf16[8,96,384]{2,1,0:T(8,128)(2,1)S(1)}, bf16[8,96,384]{2,1,0:T(8,128)(2,1)S(1)}, u32[]{:S(2)}, u32[]{:S(2)}) collective-permute-start(bf16[8,96,384]{2,1,0:T(8,128)(2,1)S(1)} %all-to-all-done.came_ref), channel_id=1, source_target_pairs={{0,16},{16,0},{1,17},{17,1},{2,18},{18,2},{3,19},{19,3},{4,20},{20... | collective-permute-start | bytes 1769480 | tf_op jit(solution)/shard_map/ppermute | solution.py:28
  44.9 4.0 %collective-permute-start.19 = (bf16[96,1008]{1,0:T(8,128)(2,1)S(1)}, bf16[96,1008]{1,0:T(8,128)(2,1)S(1)}, u32[]{:S(2)}, u32[]{:S(2)}) collective-permute-start(bf16[96,1008]{1,0:T(8,128)(2,1)S(1)} %get-tuple-element.60), channel_id=1, source_target_pairs={{0,14},{2,0},{4,2},{6,4},{8,6},{10,8},{12,10},{14,12},{1,15},{3,1}... | collective-permute-start | bytes 580616 | tf_op jit(solution)/shard_map/ppermute | solution.py:36
  55.2 2.7 %collective-permute-start.20 = (bf16[96,1008]{1,0:T(8,128)(2,1)S(1)}, bf16[96,1008]{1,0:T(8,128)(2,1)S(1)}, u32[]{:S(2)}, u32[]{:S(2)}) collective-permute-start(bf16[96,1008]{1,0:T(8,128)(2,1)S(1)} %add_convert_fusion.4), channel_id=1, source_target_pairs={{0,14},{2,0},{4,2},{6,4},{8,6},{10,8},{12,10},{14,12},{1,15},{3,1}... | collective-permute-start | bytes 580616 | tf_op jit(solution)/shard_map/ppermute | solution.py:36
  58.0 3.0 %collective-permute-start.3 = (bf16[96,1008]{1,0:T(8,128)(2,1)S(1)}, bf16[96,1008]{1,0:T(8,128)(2,1)S(1)}, u32[]{:S(2)}, u32[]{:S(2)}) collective-permute-start(bf16[96,1008]{1,0:T(8,128)(2,1)S(1)} %add_convert_fusion.9), channel_id=1, source_target_pairs={{0,14},{2,0},{4,2},{6,4},{8,6},{10,8},{12,10},{14,12},{1,15},{3,1}... | collective-permute-start | bytes 580616 | tf_op jit(solution)/shard_map/ppermute | solution.py:36
  63.7 2.7 %collective-permute-start.21 = (bf16[96,1008]{1,0:T(8,128)(2,1)S(1)}, bf16[96,1008]{1,0:T(8,128)(2,1)S(1)}, u32[]{:S(2)}, u32[]{:S(2)}) collective-permute-start(bf16[96,1008]{1,0:T(8,128)(2,1)S(1)} %add_convert_fusion.3), channel_id=1, source_target_pairs={{0,14},{2,0},{4,2},{6,4},{8,6},{10,8},{12,10},{14,12},{1,15},{3,1}... | collective-permute-start | bytes 580616 | tf_op jit(solution)/shard_map/ppermute | solution.py:36
  66.5 2.8 %collective-permute-start.4 = (bf16[96,1008]{1,0:T(8,128)(2,1)S(1)}, bf16[96,1008]{1,0:T(8,128)(2,1)S(1)}, u32[]{:S(2)}, u32[]{:S(2)}) collective-permute-start(bf16[96,1008]{1,0:T(8,128)(2,1)S(1)} %add_convert_fusion.8), channel_id=1, source_target_pairs={{0,14},{2,0},{4,2},{6,4},{8,6},{10,8},{12,10},{14,12},{1,15},{3,1}... | collective-permute-start | bytes 580616 | tf_op jit(solution)/shard_map/ppermute | solution.py:36
  72.2 5.5 %collective-permute-done.25 = bf16[96,1008]{1,0:T(8,128)(2,1)S(1)} collective-permute-done((bf16[96,1008]{1,0:T(8,128)(2,1)S(1)}, bf16[96,1008]{1,0:T(8,128)(2,1)S(1)}, u32[]{:S(2)}, u32[]{:S(2)}) %collective-permute-start.25) | collective-permute-done | bytes 193568 | tf_op jit(solution)/shard_map/ppermute | solution.py:36
  79.9 3.1 %collective-permute-done.27.refs_2_.refs_17_ = bf16[96,1008]{1,0:T(8,128)(2,1)S(1)} collective-permute-done((bf16[96,1008]{1,0:T(8,128)(2,1)S(1)}, bf16[96,1008]{1,0:T(8,128)(2,1)S(1)}, u32[]{:S(2)}, u32[]{:S(2)}) %collective-permute-start.27) | collective-permute-done | bytes 193568 | tf_op jit(solution)/shard_map/ppermute | solution.py:36
  86.3 3.1 %collective-permute-done.29.refs_4_.refs_15_ = bf16[96,1008]{1,0:T(8,128)(2,1)S(1)} collective-permute-done((bf16[96,1008]{1,0:T(8,128)(2,1)S(1)}, bf16[96,1008]{1,0:T(8,128)(2,1)S(1)}, u32[]{:S(2)}, u32[]{:S(2)}) %collective-permute-start.29) | collective-permute-done | bytes 193568 | tf_op jit(solution)/shard_map/ppermute | solution.py:36
  92.5 3.9 %collective-permute-done.31.refs_6_.refs_13_ = bf16[96,1008]{1,0:T(8,128)(2,1)S(1)} collective-permute-done((bf16[96,1008]{1,0:T(8,128)(2,1)S(1)}, bf16[96,1008]{1,0:T(8,128)(2,1)S(1)}, u32[]{:S(2)}, u32[]{:S(2)}) %collective-permute-start.31) | collective-permute-done | bytes 193568 | tf_op jit(solution)/shard_map/ppermute | solution.py:36
  96.4 3.2 %collective-permute-start.32 = (bf16[96,1008]{1,0:T(8,128)(2,1)S(1)}, bf16[96,1008]{1,0:T(8,128)(2,1)S(1)}, u32[]{:S(2)}, u32[]{:S(2)}) collective-permute-start(bf16[96,1008]{1,0:T(8,128)(2,1)S(1)} %collective-permute-done.31.refs_6_.refs_13_), channel_id=1, source_target_pairs={{0,14},{2,0},{4,2},{6,4},{8,6},{10,8},{12,10},{14,12},{1,15},{3,1}... | collective-permute-start | bytes 580616 | tf_op jit(solution)/shard_map/ppermute | solution.py:36
  104.7 9.0 %collective-permute-start.33 = (bf16[672,384]{1,0:T(8,128)(2,1)S(1)}, bf16[672,384]{1,0:T(8,128)(2,1)S(1)}, u32[]{:S(2)}, u32[]{:S(2)}) collective-permute-start(bf16[672,384]{1,0:T(8,128)(2,1)S(1)} %get-tuple-element.68), channel_id=1, source_target_pairs={{0,16},{16,0},{1,17},{17,1},{2,18},{18,2},{3,19},{19,3},{4,20},{20... | collective-permute-start | bytes 1548296 | tf_op jit(solution)/shard_map/ppermute | solution.py:28
  113.7 3.0 %collective-permute-start.12 = (bf16[96,1008]{1,0:T(8,128)(2,1)S(1)}, bf16[96,1008]{1,0:T(8,128)(2,1)S(1)}, u32[]{:S(2)}, u32[]{:S(2)}) collective-permute-start(bf16[96,1008]{1,0:T(8,128)(2,1)S(1)} %collective-permute-done.10.refs_2_.refs_9_), channel_id=1, source_target_pairs={{0,14},{2,0},{4,2},{6,4},{8,6},{10,8},{12,10},{14,12},{1,15},{3,1}... | collective-permute-start | bytes 580616 | tf_op jit(solution)/shard_map/ppermute | solution.py:36
  116.7 3.0 %collective-permute-done.12.refs_4_.refs_7_ = bf16[96,1008]{1,0:T(8,128)(2,1)S(1)} collective-permute-done((bf16[96,1008]{1,0:T(8,128)(2,1)S(1)}, bf16[96,1008]{1,0:T(8,128)(2,1)S(1)}, u32[]{:S(2)}, u32[]{:S(2)}) %collective-permute-start.12) | collective-permute-done | bytes 193568 | tf_op jit(solution)/shard_map/ppermute | solution.py:36
  119.7 3.4 %collective-permute-start.14 = (bf16[96,1008]{1,0:T(8,128)(2,1)S(1)}, bf16[96,1008]{1,0:T(8,128)(2,1)S(1)}, u32[]{:S(2)}, u32[]{:S(2)}) collective-permute-start(bf16[96,1008]{1,0:T(8,128)(2,1)S(1)} %collective-permute-done.12.refs_4_.refs_7_), channel_id=1, source_target_pairs={{0,14},{2,0},{4,2},{6,4},{8,6},{10,8},{12,10},{14,12},{1,15},{3,1}... | collective-permute-start | bytes 580616 | tf_op jit(solution)/shard_map/ppermute | solution.py:36
  129.8 3.6 %collective-permute-start.16 = (bf16[672,384]{1,0:T(8,128)(2,1)}, bf16[672,384]{1,0:T(8,128)(2,1)}, u32[]{:S(2)}, u32[]{:S(2)}) collective-permute-start(bf16[672,384]{1,0:T(8,128)(2,1)} %get-tuple-element.54), channel_id=1, source_target_pairs={{0,16},{16,0},{1,17},{17,1},{2,18},{18,2},{3,19},{19,3},{4,20},{20... | collective-permute-start | bytes 1548296 | tf_op jit(solution)/shard_map/ppermute | solution.py:28
  134.9 3.5 %all-to-all-start.3 = ((bf16[8,96,384]{2,1,0:T(8,128)(2,1)}), bf16[8,96,384]{2,1,0:T(8,128)(2,1)S(1)}, u32[]{:S(2)}, u32[]{:S(2)}) async-start(bf16[8,96,384]{2,1,0:T(8,128)(2,1)} %pair_sum.3), calls=%async_computation.3 | async-start | bytes 1179648 | tf_op jit(solution)/shard_map/all_to_all | solution.py:32
  150.7 3.1 %weight_grads.1 = (f32[192,1008]{1,0:T(8,128)S(1)}, bf16[192,1008]{1,0:T(8,128)(2,1)}) custom-call(s32[3]{0:T(128)S(1)} %pad_add_fusion.where_ref, bf16[288,768]{1,0:T(8,128)(2,1)S(1)} %copy-done.26, bf16[480,768]{1,0:T(8,128)(2,1)S(1)} %copy-done.22, bf16[288,768]{1,0:T(8,128)(2,1)S(1)} %copy-done.24, bf16[480,768]{1,0:T(8,128)(2,1)S(1)} %copy-done.20, ...), custom_call_target="tpu_custom_call" | custom-call | flops 1 | bytes 1 | tf_op jit(solution)/shard_map/weight_grads/pallas_call | solution.py:40
  157.1 7.5 %all-to-all-start.1 = ((bf16[8,96,384]{2,1,0:T(8,128)(2,1)}), bf16[8,96,384]{2,1,0:T(8,128)(2,1)S(1)}, u32[]{:S(2)}, u32[]{:S(2)}) async-start(bf16[8,96,384]{2,1,0:T(8,128)(2,1)} %pair_sum.2), calls=%async_computation.1 | async-start | bytes 1179648 | tf_op jit(solution)/shard_map/all_to_all | solution.py:32
  166.9 9.0 %all-to-all-done.1.a_ref = bf16[8,96,384]{2,1,0:T(8,128)(2,1)S(1)} async-done(((bf16[8,96,384]{2,1,0:T(8,128)(2,1)}), bf16[8,96,384]{2,1,0:T(8,128)(2,1)S(1)}, u32[]{:S(2)}, u32[]{:S(2)}) %all-to-all-start.1) | async-done | bytes 589856 | tf_op jit(solution)/shard_map/all_to_all | solution.py:32
  (168 shorter events, 65.5 us)
Async XLA Ops:
  25.4 12.6 %all-to-all-start = ((bf16[8,96,384]{2,1,0:T(8,128)(2,1)}), bf16[8,96,384]{2,1,0:T(8,128)(2,1)S(1)}, u32[]{:S(2)}, u32[]{:S(2)}) async-start(bf16[8,96,384]{2,1,0:T(8,128)(2,1)} %broadcast_in_dim.16), calls=%async_computation | async-start | bytes 1179648 | tf_op jit(solution)/shard_map/all_to_all | solution.py:32
  29.1 12.9 %collective-permute-start.18 = (bf16[8,96,384]{2,1,0:T(8,128)(2,1)S(1)}, bf16[8,96,384]{2,1,0:T(8,128)(2,1)S(1)}, u32[]{:S(2)}, u32[]{:S(2)}) collective-permute-start(bf16[8,96,384]{2,1,0:T(8,128)(2,1)S(1)} %all_to_all.20.came_ref), channel_id=1, source_target_pairs={{0,16},{16,0},{1,17},{17,1},{2,18},{18,2},{3,19},{19,3},{4,20},{20... | collective-permute-start | bytes 1769480 | tf_op jit(solution)/shard_map/ppermute | solution.py:28
  38.0 10.9 %collective-permute-start.1 = (bf16[8,96,384]{2,1,0:T(8,128)(2,1)S(1)}, bf16[8,96,384]{2,1,0:T(8,128)(2,1)S(1)}, u32[]{:S(2)}, u32[]{:S(2)}) collective-permute-start(bf16[8,96,384]{2,1,0:T(8,128)(2,1)S(1)} %all-to-all-done.came_ref), channel_id=1, source_target_pairs={{0,16},{16,0},{1,17},{17,1},{2,18},{18,2},{3,19},{19,3},{4,20},{20... | collective-permute-start | bytes 1769480 | tf_op jit(solution)/shard_map/ppermute | solution.py:28
  43.2 11.8 %collective-permute-start.22 = (bf16[96,1008]{1,0:T(8,128)(2,1)S(1)}, bf16[96,1008]{1,0:T(8,128)(2,1)S(1)}, u32[]{:S(2)}, u32[]{:S(2)}) collective-permute-start(bf16[96,1008]{1,0:T(8,128)(2,1)S(1)} %get-tuple-element.64), channel_id=1, source_target_pairs={{0,2},{2,4},{4,6},{6,8},{8,10},{10,12},{12,14},{14,0},{1,3},{3,5},... | collective-permute-start | bytes 580616 | tf_op jit(solution)/shard_map/ppermute | solution.py:36
  44.9 10.3 %collective-permute-start.19 = (bf16[96,1008]{1,0:T(8,128)(2,1)S(1)}, bf16[96,1008]{1,0:T(8,128)(2,1)S(1)}, u32[]{:S(2)}, u32[]{:S(2)}) collective-permute-start(bf16[96,1008]{1,0:T(8,128)(2,1)S(1)} %get-tuple-element.60), channel_id=1, source_target_pairs={{0,14},{2,0},{4,2},{6,4},{8,6},{10,8},{12,10},{14,12},{1,15},{3,1}... | collective-permute-start | bytes 580616 | tf_op jit(solution)/shard_map/ppermute | solution.py:36
  52.2 8.8 %collective-permute-start.6 = (bf16[96,1008]{1,0:T(8,128)(2,1)S(1)}, bf16[96,1008]{1,0:T(8,128)(2,1)S(1)}, u32[]{:S(2)}, u32[]{:S(2)}) collective-permute-start(bf16[96,1008]{1,0:T(8,128)(2,1)S(1)} %get-tuple-element.50), channel_id=1, source_target_pairs={{0,2},{2,4},{4,6},{6,8},{8,10},{10,12},{12,14},{14,0},{1,3},{3,5},... | collective-permute-start | bytes 580616 | tf_op jit(solution)/shard_map/ppermute | solution.py:36
  55.1 8.3 %collective-permute-start.23 = (bf16[96,1008]{1,0:T(8,128)(2,1)S(1)}, bf16[96,1008]{1,0:T(8,128)(2,1)S(1)}, u32[]{:S(2)}, u32[]{:S(2)}) collective-permute-start(bf16[96,1008]{1,0:T(8,128)(2,1)S(1)} %add_convert_fusion.2), channel_id=1, source_target_pairs={{0,2},{2,4},{4,6},{6,8},{8,10},{10,12},{12,14},{14,0},{1,3},{3,5},... | collective-permute-start | bytes 580616 | tf_op jit(solution)/shard_map/ppermute | solution.py:36
  55.2 8.4 %collective-permute-start.20 = (bf16[96,1008]{1,0:T(8,128)(2,1)S(1)}, bf16[96,1008]{1,0:T(8,128)(2,1)S(1)}, u32[]{:S(2)}, u32[]{:S(2)}) collective-permute-start(bf16[96,1008]{1,0:T(8,128)(2,1)S(1)} %add_convert_fusion.4), channel_id=1, source_target_pairs={{0,14},{2,0},{4,2},{6,4},{8,6},{10,8},{12,10},{14,12},{1,15},{3,1}... | collective-permute-start | bytes 580616 | tf_op jit(solution)/shard_map/ppermute | solution.py:36
  58.0 8.4 %collective-permute-start.3 = (bf16[96,1008]{1,0:T(8,128)(2,1)S(1)}, bf16[96,1008]{1,0:T(8,128)(2,1)S(1)}, u32[]{:S(2)}, u32[]{:S(2)}) collective-permute-start(bf16[96,1008]{1,0:T(8,128)(2,1)S(1)} %add_convert_fusion.9), channel_id=1, source_target_pairs={{0,14},{2,0},{4,2},{6,4},{8,6},{10,8},{12,10},{14,12},{1,15},{3,1}... | collective-permute-start | bytes 580616 | tf_op jit(solution)/shard_map/ppermute | solution.py:36
  61.1 11.0 %collective-permute-start.7 = (bf16[96,1008]{1,0:T(8,128)(2,1)S(1)}, bf16[96,1008]{1,0:T(8,128)(2,1)S(1)}, u32[]{:S(2)}, u32[]{:S(2)}) collective-permute-start(bf16[96,1008]{1,0:T(8,128)(2,1)S(1)} %add_convert_fusion.6), channel_id=1, source_target_pairs={{0,2},{2,4},{4,6},{6,8},{8,10},{10,12},{12,14},{14,0},{1,3},{3,5},... | collective-permute-start | bytes 580616 | tf_op jit(solution)/shard_map/ppermute | solution.py:36
  63.4 8.5 %collective-permute-start.24 = (bf16[96,1008]{1,0:T(8,128)(2,1)S(1)}, bf16[96,1008]{1,0:T(8,128)(2,1)S(1)}, u32[]{:S(2)}, u32[]{:S(2)}) collective-permute-start(bf16[96,1008]{1,0:T(8,128)(2,1)S(1)} %add_convert_fusion.1), channel_id=1, source_target_pairs={{0,2},{2,4},{4,6},{6,8},{8,10},{10,12},{12,14},{14,0},{1,3},{3,5},... | collective-permute-start | bytes 580616 | tf_op jit(solution)/shard_map/ppermute | solution.py:36
  63.7 8.5 %collective-permute-start.21 = (bf16[96,1008]{1,0:T(8,128)(2,1)S(1)}, bf16[96,1008]{1,0:T(8,128)(2,1)S(1)}, u32[]{:S(2)}, u32[]{:S(2)}) collective-permute-start(bf16[96,1008]{1,0:T(8,128)(2,1)S(1)} %add_convert_fusion.3), channel_id=1, source_target_pairs={{0,14},{2,0},{4,2},{6,4},{8,6},{10,8},{12,10},{14,12},{1,15},{3,1}... | collective-permute-start | bytes 580616 | tf_op jit(solution)/shard_map/ppermute | solution.py:36
  66.5 11.7 %collective-permute-start.4 = (bf16[96,1008]{1,0:T(8,128)(2,1)S(1)}, bf16[96,1008]{1,0:T(8,128)(2,1)S(1)}, u32[]{:S(2)}, u32[]{:S(2)}) collective-permute-start(bf16[96,1008]{1,0:T(8,128)(2,1)S(1)} %add_convert_fusion.8), channel_id=1, source_target_pairs={{0,14},{2,0},{4,2},{6,4},{8,6},{10,8},{12,10},{14,12},{1,15},{3,1}... | collective-permute-start | bytes 580616 | tf_op jit(solution)/shard_map/ppermute | solution.py:36
  72.1 11.8 %collective-permute-start.8 = (bf16[96,1008]{1,0:T(8,128)(2,1)S(1)}, bf16[96,1008]{1,0:T(8,128)(2,1)S(1)}, u32[]{:S(2)}, u32[]{:S(2)}) collective-permute-start(bf16[96,1008]{1,0:T(8,128)(2,1)S(1)} %add_convert_fusion.5), channel_id=1, source_target_pairs={{0,2},{2,4},{4,6},{6,8},{8,10},{10,12},{12,14},{14,0},{1,3},{3,5},... | collective-permute-start | bytes 580616 | tf_op jit(solution)/shard_map/ppermute | solution.py:36
  92.4 9.9 %collective-permute-start.30 = (bf16[96,1008]{1,0:T(8,128)(2,1)S(1)}, bf16[96,1008]{1,0:T(8,128)(2,1)S(1)}, u32[]{:S(2)}, u32[]{:S(2)}) collective-permute-start(bf16[96,1008]{1,0:T(8,128)(2,1)S(1)} %collective-permute-done.28.refs_3_.refs_16_), channel_id=1, source_target_pairs={{0,2},{2,4},{4,6},{6,8},{8,10},{10,12},{12,14},{14,0},{1,3},{3,5},... | collective-permute-start | bytes 580616 | tf_op jit(solution)/shard_map/ppermute | solution.py:36
  99.5 14.2 %collective-permute-start.10 = (bf16[96,1008]{1,0:T(8,128)(2,1)S(1)}, bf16[96,1008]{1,0:T(8,128)(2,1)S(1)}, u32[]{:S(2)}, u32[]{:S(2)}) collective-permute-start(bf16[96,1008]{1,0:T(8,128)(2,1)S(1)} %pad_maximum_fusion.refs_0_.refs_11_), channel_id=1, source_target_pairs={{0,14},{2,0},{4,2},{6,4},{8,6},{10,8},{12,10},{14,12},{1,15},{3,1}... | collective-permute-start | bytes 580616 | tf_op jit(solution)/shard_map/ppermute | solution.py:36
  99.8 16.9 %collective-permute-start.11 = (bf16[96,1008]{1,0:T(8,128)(2,1)S(1)}, bf16[96,1008]{1,0:T(8,128)(2,1)S(1)}, u32[]{:S(2)}, u32[]{:S(2)}) collective-permute-start(bf16[96,1008]{1,0:T(8,128)(2,1)S(1)} %collective-permute-done.9.refs_1_.refs_10_), channel_id=1, source_target_pairs={{0,2},{2,4},{4,6},{6,8},{8,10},{10,12},{12,14},{14,0},{1,3},{3,5},... | collective-permute-start | bytes 580616 | tf_op jit(solution)/shard_map/ppermute | solution.py:36
  104.7 28.6 %collective-permute-start.33 = (bf16[672,384]{1,0:T(8,128)(2,1)S(1)}, bf16[672,384]{1,0:T(8,128)(2,1)S(1)}, u32[]{:S(2)}, u32[]{:S(2)}) collective-permute-start(bf16[672,384]{1,0:T(8,128)(2,1)S(1)} %get-tuple-element.68), channel_id=1, source_target_pairs={{0,16},{16,0},{1,17},{17,1},{2,18},{18,2},{3,19},{19,3},{4,20},{20... | collective-permute-start | bytes 1548296 | tf_op jit(solution)/shard_map/ppermute | solution.py:28
  123.2 10.2 %collective-permute-start.34 = (bf16[96,384]{1,0:T(8,128)(2,1)S(1)}, bf16[96,384]{1,0:T(8,128)(2,1)S(1)}, u32[]{:S(2)}, u32[]{:S(2)}) collective-permute-start(bf16[96,384]{1,0:T(8,128)(2,1)S(1)} %get-tuple-element.70), channel_id=1, source_target_pairs={{0,16},{16,0},{1,17},{17,1},{2,18},{18,2},{3,19},{19,3},{4,20},{20... | collective-permute-start | bytes 221192 | tf_op jit(solution)/shard_map/ppermute | solution.py:28
  129.8 25.4 %collective-permute-start.16 = (bf16[672,384]{1,0:T(8,128)(2,1)}, bf16[672,384]{1,0:T(8,128)(2,1)}, u32[]{:S(2)}, u32[]{:S(2)}) collective-permute-start(bf16[672,384]{1,0:T(8,128)(2,1)} %get-tuple-element.54), channel_id=1, source_target_pairs={{0,16},{16,0},{1,17},{17,1},{2,18},{18,2},{3,19},{19,3},{4,20},{20... | collective-permute-start | bytes 1548296 | tf_op jit(solution)/shard_map/ppermute | solution.py:28
  134.9 22.3 %all-to-all-start.3 = ((bf16[8,96,384]{2,1,0:T(8,128)(2,1)}), bf16[8,96,384]{2,1,0:T(8,128)(2,1)S(1)}, u32[]{:S(2)}, u32[]{:S(2)}) async-start(bf16[8,96,384]{2,1,0:T(8,128)(2,1)} %pair_sum.3), calls=%async_computation.3 | async-start | bytes 1179648 | tf_op jit(solution)/shard_map/all_to_all | solution.py:32
  138.4 16.7 %collective-permute-start.17 = (bf16[96,384]{1,0:T(8,128)(2,1)}, bf16[96,384]{1,0:T(8,128)(2,1)S(1)}, u32[]{:S(2)}, u32[]{:S(2)}) collective-permute-start(bf16[96,384]{1,0:T(8,128)(2,1)} %copy-done.28), channel_id=1, source_target_pairs={{0,16},{16,0},{1,17},{17,1},{2,18},{18,2},{3,19},{19,3},{4,20},{20... | collective-permute-start | bytes 221192 | tf_op jit(solution)/shard_map/ppermute | solution.py:28
  154.7 11.1 %collective-permute-start.36 = (bf16[192,1008]{1,0:T(8,128)(2,1)}, bf16[192,1008]{1,0:T(8,128)(2,1)}, u32[]{:S(2)}, u32[]{:S(2)}) collective-permute-start(bf16[192,1008]{1,0:T(8,128)(2,1)} %get-tuple-element.80), channel_id=1, source_target_pairs={{0,1},{1,0},{2,3},{3,2},{4,5},{5,4},{6,7},{7,6},{8,9},{9,8},{10,11... | collective-permute-start | bytes 1161224 | tf_op jit(solution)/shard_map/ppermute | solution.py:297
  157.1 18.7 %all-to-all-start.1 = ((bf16[8,96,384]{2,1,0:T(8,128)(2,1)}), bf16[8,96,384]{2,1,0:T(8,128)(2,1)S(1)}, u32[]{:S(2)}, u32[]{:S(2)}) async-start(bf16[8,96,384]{2,1,0:T(8,128)(2,1)} %pair_sum.2), calls=%async_computation.1 | async-start | bytes 1179648 | tf_op jit(solution)/shard_map/all_to_all | solution.py:32
  (49 other events, 267.6 us)

commit v2 on v0

v2 whole, which is shorter than its diff:
```python
import functools

import jax
import jax.numpy as jnp
from jax import lax
from jax.experimental import pallas as pl
from jax.experimental.pallas import tpu as pltpu
from jax.sharding import Mesh
from jax.sharding import PartitionSpec as P

BF16 = jnp.bfloat16
F32 = jnp.float32
XS, YS, CORES, RING = 4, 2, 2, 8
CHIPS = XS * YS
FIRST, LAST = 640, 768
VMEM_LIMIT = 40 * 1024 * 1024
WHOLE = pl.BlockSpec(memory_space=pltpu.VMEM)
SCALARS = pl.BlockSpec(memory_space=pltpu.SMEM)


def dot(left, right, left_dim, right_dim):
    return lax.dot_general(
        left, right, (((left_dim,), (right_dim,)), ((), ())), preferred_element_type=F32
    )


def core_swap(x):
    return lax.ppermute(x, "core", [(0, 1), (1, 0)])


def among_chips(x):
    return lax.all_to_all(x, ("x", "y"), 0, 0, tiled=True)


def ring(x, by):
    return lax.ppermute(x, "tensor", [(z, (z + by) % RING) for z in range(RING)])


def local_call(body, name, out_shape, operands, scratch=()):
    return pl.pallas_call(
        body,
        out_shape=out_shape,
        in_specs=[SCALARS] + [WHOLE] * len(operands[1:]),
        out_specs=jax.tree.map(lambda _: WHOLE, out_shape),
        scratch_shapes=scratch,
        compiler_params=pltpu.CompilerParams(vmem_limit_bytes=VMEM_LIMIT),
        cost_estimate=pl.CostEstimate(flops=1, bytes_accessed=1, transcendentals=0),
        name=name,
    )(*operands)


def column(row):
    size = row.shape[1]
    same = lax.broadcasted_iota(jnp.int32, (size, size), 0) == lax.broadcasted_iota(
        jnp.int32, (size, size), 1
    )
    return jnp.sum(jnp.where(same, row, 0.0), axis=1, keepdims=True)


def routes(count_ref, index_ref, gate_ref, token_count):
    size = index_ref.shape[1]
    live = lax.broadcasted_iota(jnp.int32, (1, size), 1) < count_ref[0]
    token = lax.broadcasted_iota(jnp.int32, (token_count, size), 0)
    place = jnp.where(token == index_ref[...], 1.0, 0.0).astype(BF16)
    weight = column(jnp.where(live, gate_ref[...], 0.0))
    return place, weight, column(jnp.where(live, 1.0, 0.0))


def gather_body(count_ref, tokens_ref, grads_ref, index_ref, gate_ref, out_ref):
    token_count, width = tokens_ref.shape
    place, weight, _ = routes(count_ref, index_ref, gate_ref, token_count)
    rows = dot(place, tokens_ref[...], 0, 0).astype(BF16)
    grads = (weight * dot(place, grads_ref[...], 0, 0)).astype(BF16)
    for n in range(CHIPS):
        out_ref[n, :, :width] = rows
        out_ref[n, :, width:] = grads


def pre_body(deltas, where_ref, rows_ref, w_rows_ref, w_grads_ref, payload_ref, *refs):
    here = where_ref[0]
    size = rows_ref.shape[1]
    width = rows_ref.shape[2] // 2
    for n, delta in enumerate(deltas):
        payload_ref[n * size : (n + 1) * size, :] = rows_ref[lax.rem(here + delta, RING)]
    by_rows = dot(payload_ref[:, :width], w_rows_ref[...], 1, 1)
    by_grads = dot(payload_ref[:, width:], w_grads_ref[...], 1, 1)
    mixed = by_rows[:, FIRST:] + by_grads[:, : LAST - FIRST]
    for n, ref in enumerate(refs):
        rows, kind = slice(n * size, (n + 1) * size), ref.dtype
        ref[:, :FIRST] = by_rows[rows, :FIRST].astype(kind)
        ref[:, FIRST:LAST] = mixed[rows].astype(kind)
        ref[:, LAST:] = by_grads[rows, LAST - FIRST :].astype(kind)


def join(refs, to_ref):
    size = refs[0].shape[0]
    for n, ref in enumerate(refs):
        to_ref[n * size : (n + 1) * size, :] = ref[...]


def out_body(where_ref, w_rows_ref, w_grads_ref, *refs):
    keep_ref, give_ref, acts_ref = refs[-3:]
    join(refs[:-3], acts_ref)
    size, width = keep_ref.shape[0], w_rows_ref.shape[1]
    out = dot(acts_ref[:, FIRST:], w_grads_ref[...], 1, 0)
    back = dot(acts_ref[:, :LAST], w_rows_ref[...], 1, 0)
    keep_ref[:, :width] = out[:size]
    keep_ref[:, width:] = back[:size]
    give_ref[:, :width] = out[size:].astype(BF16)
    give_ref[:, width:] = back[size:].astype(BF16)


def weight_body(block, where_ref, *refs):
    dp = where_ref[1]
    payload_refs = refs[:4]
    keep_ref, give_ref, acts_ref = refs[-3:]
    join(refs[4:-3], acts_ref)
    part = keep_ref.shape[0]
    width = 2 * part

    def product(cols, units):
        total, at = None, 0
        for ref in payload_refs:
            term = dot(ref[:, cols], acts_ref[at : at + ref.shape[0], units], 0, 0)
            total = term if total is None else total + term
            at += ref.shape[0]
        return total

    by_rows = product(slice(0, width), slice(0, LAST))
    by_grads = product(slice(width, 2 * width), slice(FIRST, acts_ref.shape[1]))
    unit = FIRST + lax.broadcasted_iota(jnp.int32, (part, LAST - FIRST), 1)
    for cols in (slice(0, FIRST), slice(FIRST, LAST), slice(LAST, acts_ref.shape[1])):
        halves = []
        for rows in (slice(0, part), slice(part, width)):
            if cols.stop == FIRST:
                halves.append(by_rows[rows, :FIRST])
            elif cols.start == FIRST:
                halves.append(
                    jnp.where(
                        unit < 2 * block, by_rows[rows, FIRST:], by_grads[rows, : LAST - FIRST]
                    )
                )
            else:
                halves.append(by_grads[rows, LAST - FIRST :])
        keep_ref[:, cols] = jnp.where(dp == 0, halves[0], halves[1])
        give_ref[:, cols] = jnp.where(dp == 0, halves[1], halves[0]).astype(BF16)


def pair_body(deltas, where_ref, keep_ref, got_ref, keep_last_ref, got_last_ref, out_ref):
    here = where_ref[0]
    size = out_ref.shape[1]
    for n, delta in enumerate(deltas):
        rows = slice(n * size, (n + 1) * size)
        out_ref[lax.rem(here + delta, RING)] = (
            keep_ref[rows] + got_ref[rows].astype(F32)
        ).astype(BF16)
    out_ref[lax.rem(here + RING // 2, RING)] = (
        keep_last_ref[...] + got_last_ref[...].astype(F32)
    ).astype(BF16)


def scatter_body(count_ref, came_ref, index_ref, gate_ref, mixed_ref, grad_ref):
    total = came_ref[0].astype(F32)
    for n in range(1, CHIPS):
        total = total + came_ref[n].astype(F32)
    token_count, width = mixed_ref.shape
    place, weight, live = routes(count_ref, index_ref, gate_ref, token_count)
    out_rows = (weight * total[:, :width]).astype(BF16)
    back_rows = jnp.where(live > 0.0, total[:, width:], 0.0).astype(BF16)
    mixed_ref[...] = dot(place, out_rows, 1, 0).astype(BF16)
    grad_ref[...] = dot(place, back_rows, 1, 0).astype(BF16)


def on_device(
    tokens, out_grad, gate_weight, up_weight, down_weight, route_count, route_index, route_gate
):
    capacity = route_index.shape[0]
    token_count, width = tokens.shape
    block = gate_weight.shape[0]
    units = 3 * block
    here = lax.axis_index("tensor")
    where = jnp.stack([here, lax.axis_index("dp")]).astype(jnp.int32)
    routing = [route_index[None, :], route_gate[None, :]]

    w_rows = jnp.concatenate(
        [gate_weight, up_weight, jnp.zeros((LAST - 2 * block, width), BF16)], axis=0
    )
    w_grads = jnp.concatenate(
        [jnp.zeros((2 * block - FIRST, width), BF16), down_weight], axis=0
    )

    copies = local_call(
        gather_body,
        "gather_rows",
        jax.ShapeDtypeStruct((CHIPS, capacity, 2 * width), BF16),
        [route_count, tokens, out_grad] + routing,
    )
    came = among_chips(copies)
    pre = {}
    payloads = []
    first, rest = (4, 3, 5), (2, 6, 1, 7, 0)
    for h, rows in enumerate((came, core_swap(came))):
        for deltas, name in ((first, "pre_first"), (rest, "pre_rest")):
            shapes = [jax.ShapeDtypeStruct((len(deltas) * capacity, 2 * width), BF16)]
            for delta in deltas:
                starts = delta == 4 or (delta, h) in ((3, 0), (5, 1))
                shapes.append(jax.ShapeDtypeStruct((capacity, units), BF16 if starts else F32))
            payload, *blocks = local_call(
                functools.partial(pre_body, deltas), name, shapes, [where, rows, w_rows, w_grads]
            )
            payloads.append(payload)
            pre.update({(delta, h): part for delta, part in zip(deltas, blocks)})

    own_left, own_right = ring(pre[4, 0], -1), ring(pre[3, 0], 1)
    own_left, own_right, payloads[2] = lax.optimization_barrier(
        (own_left, own_right, payloads[2])
    )
    sums = []
    for h, ways in (
        (0, ((own_left, (5, 6, 7), -1), (own_right, (2, 1), 1))),
        (1, ((None, (5, 6, 7), -1), (None, (4, 3, 2, 1), 1))),
    ):
        total = pre[0, h]
        for moving, path, by in ways:
            for delta in path:
                block_sum = pre[delta, h]
                if moving is not None:
                    block_sum = block_sum + moving.astype(F32)
                moving = ring(block_sum.astype(BF16), by)
            total = total + moving.astype(F32)
        sums.append(total)

    acts_own = []
    for total in sums:
        gate_pre, up_pre, d_hidden = (
            total[:, :block],
            total[:, block : 2 * block],
            total[:, 2 * block :],
        )
        sigmoid_gate = jax.nn.sigmoid(gate_pre)
        activated = gate_pre * sigmoid_gate
        hidden = (activated * up_pre).astype(BF16)
        d_gate = (
            d_hidden * up_pre * sigmoid_gate * (1.0 + gate_pre * (1.0 - sigmoid_gate))
        ).astype(BF16)
        d_up = (d_hidden * activated).astype(BF16)
        acts_own.append(jnp.concatenate([d_gate, d_up, hidden], axis=1))

    halves = {0: acts_own}
    right = list(acts_own)
    left = list(acts_own)
    for step in (1, 2, 3):
        right = [ring(a, 1) for a in right]
        left = [ring(a, -1) for a in left]
        halves[RING - step] = right
        halves[step] = left
    halves[4] = [ring(right[0], 1), ring(left[1], -1)]

    near, far = (0, 7, 1, 6, 2, 5, 3), (4,)
    kept, given = [], []
    for deltas, name in ((near, "out_near"), (far, "out_far")):
        shape = (len(deltas) * capacity, 2 * width)
        keep, give = local_call(
            out_body,
            name,
            [jax.ShapeDtypeStruct(shape, F32), jax.ShapeDtypeStruct(shape, BF16)],
            [where, w_rows, w_grads] + [halves[delta][h] for h in range(2) for delta in deltas],
            [pltpu.VMEM((2 * len(deltas) * capacity, units), BF16)],
        )
        kept.append(keep)
        given.append(give)
    swapped = [core_swap(give) for give in lax.optimization_barrier(given)]

    part = width // 2
    pieces = [halves[delta][h] for h in range(2) for delta in first + rest]
    keep_w, give_w = local_call(
        functools.partial(weight_body, block),
        "weight_grads",
        [jax.ShapeDtypeStruct((part, units), F32), jax.ShapeDtypeStruct((part, units), BF16)],
        [where] + payloads + pieces,
        [pltpu.VMEM((len(pieces) * capacity, units), BF16)],
    )
    swapped, give_w = lax.optimization_barrier((swapped, give_w))
    got_w = lax.ppermute(give_w, "dp", [(0, 1), (1, 0)])
    by_chip = local_call(
        functools.partial(pair_body, near),
        "pair_sum",
        jax.ShapeDtypeStruct((CHIPS, capacity, 2 * width), BF16),
        [where, kept[0], swapped[0], kept[1], swapped[1]],
    )
    arrived = among_chips(by_chip)
    mixed, input_grad = local_call(
        scatter_body,
        "scatter_rows",
        [jax.ShapeDtypeStruct((token_count, width), BF16)] * 2,
        [route_count, arrived] + routing,
    )
    grads_w = keep_w + got_w.astype(F32)
    return (
        mixed,
        input_grad,
        grads_w[:, :block].T,
        grads_w[:, block : 2 * block].T,
        grads_w[:, 2 * block :].T,
    )


def solution(mesh):
    ways = (("x", "y", "core"), "tensor", "dp")
    chips = Mesh(mesh.devices.reshape(XS, YS, CORES, RING, 2), ways[0] + ways[1:])
    expert, tensor, dp = ways
    tokens = P(expert + (dp,), tensor)
    weight = P(expert, tensor)
    slots = P(expert + (dp,))
    grad = P(expert, (tensor, dp))
    return jax.shard_map(
        on_device,
        mesh=chips,
        in_specs=(tokens, tokens, weight, weight, weight, slots, slots, slots),
        out_specs=(tokens, tokens, grad, grad, grad),
        check_vma=False,
    )
```

time: 151 us -> 146 us (0.967)
  waiting for transfers between devices: 55.7 us -> 48.6 us
  local copies, waits for them, and re-layouts: 1.54 us -> 4.41 us
  blocking collectives: 22.1 us -> 24.4 us
  matrix products: 2.03 us -> 0 us
    ppermute x28, waiting for transfers between devices: 30.9 us -> 26.7 us  [ring(): lax.ppermute(x, 'tensor', [(z, (z + by) % RING) for z in range(RING)])]
    unnamed x12 -> x18, local copies, waits for them, and re-layouts: 0.04 us -> 3.19 us
    ppermute x4 -> x3, waiting for transfers between devices: 3.01 us -> 0.01 us  [core_swap(): return lax.ppermute(x, 'core', [(0, 1), (1, 0)])]
    all_to_all x1, blocking collectives: 22.1 us -> 24.4 us  [among_chips(): return lax.all_to_all(x, ('x', 'y'), 0, 0, tiled=True)]
    dot_general x2 -> x0, matrix products: 2.03 us -> none  [dot(): lax.dot_general(left, right, (((left_dim,), (right_dim,)), ((), ())), pre...]
    ppermute x4 -> x3, starting transfers between devices: 12.6 us -> 10.8 us  [core_swap(): return lax.ppermute(x, 'core', [(0, 1), (1, 0)])]
    pallas_call x7 -> x10, Pallas kernels: 13.6 us -> 14.2 us  [local_call(): pl.pallas_call(body, out_shape=out_shape, in_specs=[SCALARS] + [WHOLE] *...]
  transfers between devices with their start and end apart: 34 -> 33, of which waited for: 20 -> 16; matrix products, arithmetic and copies ran while one was open for 2% -> 2% of each run, Pallas kernels for 5% -> 7%
where the time goes in v2:
time: 146 us; the launch traced here: 145 us
  starting transfers between devices  50.7 us (35%)
  waiting for transfers between devices  48.6 us (33%)
  blocking collectives  24.4 us (17%)
  Pallas kernels  14.2 us (10%)
  local copies, waits for them, and re-layouts  4.41 us (3%)
  between operations  1.65 us (1%)
  other arithmetic  1.5 us (1%)
    ppermute x28, starting transfers between devices, ring(): lax.ppermute(x, 'tensor', [(z, (z + by) % RING) for z in range(RING)])  35.8 us
    ppermute x28, waiting for transfers between devices, ring(): lax.ppermute(x, 'tensor', [(z, (z + by) % RING) for z in range(RING)])  26.7 us
    all_to_all x1, blocking collectives, among_chips(): return lax.all_to_all(x, ('x', 'y'), 0, 0, tiled=True)  24.4 us
    ppermute x1, waiting for transfers between devices, on_device(): got_w = lax.ppermute(give_w, 'dp', [(0, 1), (1, 0)])  21.9 us
    pallas_call x10, Pallas kernels, local_call(): pl.pallas_call(body, out_shape=out_shape, in_specs=[SCALARS] + [WHOLE] *...  14.2 us
    ppermute x3, starting transfers between devices, core_swap(): return lax.ppermute(x, 'core', [(0, 1), (1, 0)])  10.8 us
    all_to_all x1, starting transfers between devices, among_chips(): return lax.all_to_all(x, ('x', 'y'), 0, 0, tiled=True)  3.56 us
    unnamed x18, local copies, waits for them, and re-layouts  3.19 us
  transfers between devices with their start and end apart: 33, of which 16 were waited for; matrix products, arithmetic and copies ran while one was open for 2% of the time, Pallas kernels for 7%

profile of v2, /device:TPU:1, one launch (start us, length us, event | category | flops | bytes accessed | tf_op | source)
XLA Modules:
  0.0 145.4 jit_solution(3342299854427348080)
XLA Ops:
  4.8 24.4 %all_to_all.10.rows_ref = bf16[8,96,768]{2,1,0:T(8,128)(2,1)S(1)} all-to-all(bf16[8,96,768]{2,1,0:T(8,128)(2,1)S(1)} %gather_rows.1), channel_id=1, replica_groups=mesh['x'=4,'y'=2,'core'=2,'tensor'=8,'dp'=2] {'x','y'}, dimensions={0} | all-to-all | bytes 2359296 | tf_op jit(solution)/shard_map/all_to_all | solution.py:32
  29.2 2.4 %collective-permute-start.2 = (bf16[8,96,768]{2,1,0:T(8,128)(2,1)S(1)}, bf16[8,96,768]{2,1,0:T(8,128)(2,1)S(1)}, u32[]{:S(2)}, u32[]{:S(2)}) collective-permute-start(bf16[8,96,768]{2,1,0:T(8,128)(2,1)S(1)} %all_to_all.10.rows_ref), channel_id=1, source_target_pairs={{0,16},{16,0},{1,17},{17,1},{2,18},{18,2},{3,19},{19,3},{4,20},{20... | collective-permute-start | bytes 3538952 | tf_op jit(solution)/shard_map/ppermute | solution.py:28
  33.1 5.7 %collective-permute-start = (bf16[96,1008]{1,0:T(8,128)(2,1)S(1)}, bf16[96,1008]{1,0:T(8,128)(2,1)S(1)}, u32[]{:S(2)}, u32[]{:S(2)}) collective-permute-start(bf16[96,1008]{1,0:T(8,128)(2,1)S(1)} %get-tuple-element.45), channel_id=1, source_target_pairs={{0,14},{2,0},{4,2},{6,4},{8,6},{10,8},{12,10},{14,12},{1,15},{3,1}... | collective-permute-start | bytes 580616 | tf_op jit(solution)/shard_map/ppermute | solution.py:36
  41.2 2.8 %collective-permute-start.14 = (bf16[96,1008]{1,0:T(8,128)(2,1)S(1)}, bf16[96,1008]{1,0:T(8,128)(2,1)S(1)}, u32[]{:S(2)}, u32[]{:S(2)}) collective-permute-start(bf16[96,1008]{1,0:T(8,128)(2,1)S(1)} %get-tuple-element.55), channel_id=1, source_target_pairs={{0,14},{2,0},{4,2},{6,4},{8,6},{10,8},{12,10},{14,12},{1,15},{3,1}... | collective-permute-start | bytes 580616 | tf_op jit(solution)/shard_map/ppermute | solution.py:36
  44.0 2.2 %collective-permute-done.1 = bf16[96,1008]{1,0:T(8,128)(2,1)S(1)} collective-permute-done((bf16[96,1008]{1,0:T(8,128)(2,1)S(1)}, bf16[96,1008]{1,0:T(8,128)(2,1)S(1)}, u32[]{:S(2)}, u32[]{:S(2)}) %collective-permute-start.1) | collective-permute-done | bytes 193568 | tf_op jit(solution)/shard_map/ppermute | solution.py:36
  52.0 3.5 %collective-permute-start.4 = (bf16[96,1008]{1,0:T(8,128)(2,1)S(1)}, bf16[96,1008]{1,0:T(8,128)(2,1)S(1)}, u32[]{:S(2)}, u32[]{:S(2)}) collective-permute-start(bf16[96,1008]{1,0:T(8,128)(2,1)S(1)} %add_convert_fusion.8), channel_id=1, source_target_pairs={{0,14},{2,0},{4,2},{6,4},{8,6},{10,8},{12,10},{14,12},{1,15},{3,1}... | collective-permute-start | bytes 580616 | tf_op jit(solution)/shard_map/ppermute | solution.py:36
  55.7 2.7 %collective-permute-start.15 = (bf16[96,1008]{1,0:T(8,128)(2,1)S(1)}, bf16[96,1008]{1,0:T(8,128)(2,1)S(1)}, u32[]{:S(2)}, u32[]{:S(2)}) collective-permute-start(bf16[96,1008]{1,0:T(8,128)(2,1)S(1)} %add_convert_fusion.4), channel_id=1, source_target_pairs={{0,14},{2,0},{4,2},{6,4},{8,6},{10,8},{12,10},{14,12},{1,15},{3,1}... | collective-permute-start | bytes 580616 | tf_op jit(solution)/shard_map/ppermute | solution.py:36
  58.4 3.4 %collective-permute-start.5 = (bf16[96,1008]{1,0:T(8,128)(2,1)S(1)}, bf16[96,1008]{1,0:T(8,128)(2,1)S(1)}, u32[]{:S(2)}, u32[]{:S(2)}) collective-permute-start(bf16[96,1008]{1,0:T(8,128)(2,1)S(1)} %add_convert_fusion.7), channel_id=1, source_target_pairs={{0,14},{2,0},{4,2},{6,4},{8,6},{10,8},{12,10},{14,12},{1,15},{3,1}... | collective-permute-start | bytes 580616 | tf_op jit(solution)/shard_map/ppermute | solution.py:36
  62.3 3.6 %collective-permute-start.16 = (bf16[96,1008]{1,0:T(8,128)(2,1)S(1)}, bf16[96,1008]{1,0:T(8,128)(2,1)S(1)}, u32[]{:S(2)}, u32[]{:S(2)}) collective-permute-start(bf16[96,1008]{1,0:T(8,128)(2,1)S(1)} %add_convert_fusion.3), channel_id=1, source_target_pairs={{0,14},{2,0},{4,2},{6,4},{8,6},{10,8},{12,10},{14,12},{1,15},{3,1}... | collective-permute-start | bytes 580616 | tf_op jit(solution)/shard_map/ppermute | solution.py:36
  65.9 1.8 %collective-permute-done.19 = bf16[96,1008]{1,0:T(8,128)(2,1)S(1)} collective-permute-done((bf16[96,1008]{1,0:T(8,128)(2,1)S(1)}, bf16[96,1008]{1,0:T(8,128)(2,1)S(1)}, u32[]{:S(2)}, u32[]{:S(2)}) %collective-permute-start.19) | collective-permute-done | bytes 193568 | tf_op jit(solution)/shard_map/ppermute | solution.py:36
  68.3 2.3 %collective-permute-done.16 = bf16[96,1008]{1,0:T(8,128)(2,1)S(1)} collective-permute-done((bf16[96,1008]{1,0:T(8,128)(2,1)S(1)}, bf16[96,1008]{1,0:T(8,128)(2,1)S(1)}, u32[]{:S(2)}, u32[]{:S(2)}) %collective-permute-start.16) | collective-permute-done | bytes 193568 | tf_op jit(solution)/shard_map/ppermute | solution.py:36
  70.6 3.6 %collective-permute-done.20 = bf16[96,1008]{1,0:T(8,128)(2,1)S(1)} collective-permute-done((bf16[96,1008]{1,0:T(8,128)(2,1)S(1)}, bf16[96,1008]{1,0:T(8,128)(2,1)S(1)}, u32[]{:S(2)}, u32[]{:S(2)}) %collective-permute-start.20) | collective-permute-done | bytes 193568 | tf_op jit(solution)/shard_map/ppermute | solution.py:36
  77.6 1.9 %collective-permute-done.22.refs_9_.refs_17_ = bf16[96,1008]{1,0:T(8,128)(2,1)S(1)} collective-permute-done((bf16[96,1008]{1,0:T(8,128)(2,1)S(1)}, bf16[96,1008]{1,0:T(8,128)(2,1)S(1)}, u32[]{:S(2)}, u32[]{:S(2)}) %collective-permute-start.22) | collective-permute-done | bytes 193568 | tf_op jit(solution)/shard_map/ppermute | solution.py:36
  83.1 3.0 %collective-permute-done.10.refs_3_.refs_8_ = bf16[96,1008]{1,0:T(8,128)(2,1)S(1)} collective-permute-done((bf16[96,1008]{1,0:T(8,128)(2,1)S(1)}, bf16[96,1008]{1,0:T(8,128)(2,1)S(1)}, u32[]{:S(2)}, u32[]{:S(2)}) %collective-permute-start.10) | collective-permute-done | bytes 193568 | tf_op jit(solution)/shard_map/ppermute | solution.py:36
  86.1 2.7 %collective-permute-start.26 = (bf16[96,1008]{1,0:T(8,128)(2,1)S(1)}, bf16[96,1008]{1,0:T(8,128)(2,1)S(1)}, u32[]{:S(2)}, u32[]{:S(2)}) collective-permute-start(bf16[96,1008]{1,0:T(8,128)(2,1)S(1)} %collective-permute-done.24.refs_11_.refs_15_), channel_id=1, source_target_pairs={{0,14},{2,0},{4,2},{6,4},{8,6},{10,8},{12,10},{14,12},{1,15},{3,1}... | collective-permute-start | bytes 580616 | tf_op jit(solution)/shard_map/ppermute | solution.py:36
  88.8 2.0 %collective-permute-start.13 = (bf16[96,1008]{1,0:T(8,128)(2,1)S(1)}, bf16[96,1008]{1,0:T(8,128)(2,1)S(1)}, u32[]{:S(2)}, u32[]{:S(2)}) collective-permute-start(bf16[96,1008]{1,0:T(8,128)(2,1)S(1)} %collective-permute-done.11.refs_4_.refs_7_), channel_id=1, source_target_pairs={{0,14},{2,0},{4,2},{6,4},{8,6},{10,8},{12,10},{14,12},{1,15},{3,1}... | collective-permute-start | bytes 580616 | tf_op jit(solution)/shard_map/ppermute | solution.py:36
  91.1 3.9 %collective-permute-done.12.refs_5_.refs_6_ = bf16[96,1008]{1,0:T(8,128)(2,1)S(1)} collective-permute-done((bf16[96,1008]{1,0:T(8,128)(2,1)S(1)}, bf16[96,1008]{1,0:T(8,128)(2,1)S(1)}, u32[]{:S(2)}, u32[]{:S(2)}) %collective-permute-start.12) | collective-permute-done | bytes 193568 | tf_op jit(solution)/shard_map/ppermute | solution.py:36
  95.0 2.7 %collective-permute-start.28 = (bf16[96,1008]{1,0:T(8,128)(2,1)S(1)}, bf16[96,1008]{1,0:T(8,128)(2,1)S(1)}, u32[]{:S(2)}, u32[]{:S(2)}) collective-permute-start(bf16[96,1008]{1,0:T(8,128)(2,1)S(1)} %collective-permute-done.26.refs_13_), channel_id=1, source_target_pairs={{0,14},{2,0},{4,2},{6,4},{8,6},{10,8},{12,10},{14,12},{1,15},{3,1}... | collective-permute-start | bytes 580616 | tf_op jit(solution)/shard_map/ppermute | solution.py:36
  97.7 2.4 %out_near.1 = (f32[672,768]{1,0:T(8,128)S(1)}, bf16[672,768]{1,0:T(8,128)(2,1)S(1)}) custom-call(s32[2]{0:T(128)S(1)} %pad_add_fusion.where_ref, bf16[768,384]{1,0:T(8,128)(2,1)S(1)} %maximum_maximum_fusion.w_rows_ref, bf16[368,384]{1,0:T(8,128)(2,1)S(1)} %concatenate.13.w_grads_ref, bf16[96,1008]{1,0:T(8,128)(2,1)S(1)} %pad_maximum_fusion.refs_0_.refs_11_, ...), custom_call_target="tpu_custom_call" | custom-call | flops 1 | bytes 1 | tf_op jit(solution)/shard_map/out_near/pallas_call | solution.py:40
  100.1 3.0 %collective-permute-done.27.refs_0_.refs_4_ = bf16[96,1008]{1,0:T(8,128)(2,1)S(1)} collective-permute-done((bf16[96,1008]{1,0:T(8,128)(2,1)S(1)}, bf16[96,1008]{1,0:T(8,128)(2,1)S(1)}, u32[]{:S(2)}, u32[]{:S(2)}) %collective-permute-start.27) | collective-permute-done | bytes 193568 | tf_op jit(solution)/shard_map/ppermute | solution.py:36
  104.1 8.3 %collective-permute-start.29 = (bf16[672,768]{1,0:T(8,128)(2,1)S(1)}, bf16[672,768]{1,0:T(8,128)(2,1)S(1)}, u32[]{:S(2)}, u32[]{:S(2)}) collective-permute-start(bf16[672,768]{1,0:T(8,128)(2,1)S(1)} %get-tuple-element.63), channel_id=1, source_target_pairs={{0,16},{16,0},{1,17},{17,1},{2,18},{18,2},{3,19},{19,3},{4,20},{20... | collective-permute-start | bytes 3096584 | tf_op jit(solution)/shard_map/ppermute | solution.py:28
  112.6 2.8 %weight_grads.1 = (f32[192,1008]{1,0:T(8,128)S(1)}, bf16[192,1008]{1,0:T(8,128)(2,1)S(1)}) custom-call(s32[2]{0:T(128)S(1)} %pad_add_fusion.where_ref, bf16[288,768]{1,0:T(8,128)(2,1)S(1)} %get-tuple-element.65.refs_0_, bf16[480,768]{1,0:T(8,128)(2,1)S(1)} %get-tuple-element.66.refs_1_, bf16[288,768]{1,0:T(8,128)(2,1)S(1)} %get-tuple-element.67.refs_2_, ...), custom_call_target="tpu_custom_call" | custom-call | flops 1 | bytes 1 | tf_op jit(solution)/shard_map/weight_grads/pallas_call | solution.py:40
  117.2 3.6 %all-to-all-start.1 = ((bf16[8,96,768]{2,1,0:T(8,128)(2,1)}), bf16[8,96,768]{2,1,0:T(8,128)(2,1)S(1)}, u32[]{:S(2)}, u32[]{:S(2)}) async-start(bf16[8,96,768]{2,1,0:T(8,128)(2,1)} %pair_sum.1), calls=%async_computation.1 | async-start | bytes 2359296 | tf_op jit(solution)/shard_map/all_to_all | solution.py:32
  121.2 21.9 %collective-permute-done.31 = bf16[192,1008]{1,0:T(8,128)(2,1)S(1)} collective-permute-done((bf16[192,1008]{1,0:T(8,128)(2,1)S(1)}, bf16[192,1008]{1,0:T(8,128)(2,1)S(1)}, u32[]{:S(2)}, u32[]{:S(2)}) %collective-permute-start.31) | collective-permute-done | bytes 387104 | tf_op jit(solution)/shard_map/ppermute | solution.py:284
  (94 shorter events, 27.2 us)
Async XLA Ops:
  29.2 10.9 %collective-permute-start.2 = (bf16[8,96,768]{2,1,0:T(8,128)(2,1)S(1)}, bf16[8,96,768]{2,1,0:T(8,128)(2,1)S(1)}, u32[]{:S(2)}, u32[]{:S(2)}) collective-permute-start(bf16[8,96,768]{2,1,0:T(8,128)(2,1)S(1)} %all_to_all.10.rows_ref), channel_id=1, source_target_pairs={{0,16},{16,0},{1,17},{17,1},{2,18},{18,2},{3,19},{19,3},{4,20},{20... | collective-permute-start | bytes 3538952 | tf_op jit(solution)/shard_map/ppermute | solution.py:28
  33.1 10.9 %collective-permute-start = (bf16[96,1008]{1,0:T(8,128)(2,1)S(1)}, bf16[96,1008]{1,0:T(8,128)(2,1)S(1)}, u32[]{:S(2)}, u32[]{:S(2)}) collective-permute-start(bf16[96,1008]{1,0:T(8,128)(2,1)S(1)} %get-tuple-element.45), channel_id=1, source_target_pairs={{0,14},{2,0},{4,2},{6,4},{8,6},{10,8},{12,10},{14,12},{1,15},{3,1}... | collective-permute-start | bytes 580616 | tf_op jit(solution)/shard_map/ppermute | solution.py:36
  38.8 7.4 %collective-permute-start.1 = (bf16[96,1008]{1,0:T(8,128)(2,1)S(1)}, bf16[96,1008]{1,0:T(8,128)(2,1)S(1)}, u32[]{:S(2)}, u32[]{:S(2)}) collective-permute-start(bf16[96,1008]{1,0:T(8,128)(2,1)S(1)} %get-tuple-element.46), channel_id=1, source_target_pairs={{0,2},{2,4},{4,6},{6,8},{8,10},{10,12},{12,14},{14,0},{1,3},{3,5},... | collective-permute-start | bytes 580616 | tf_op jit(solution)/shard_map/ppermute | solution.py:36
  41.2 14.4 %collective-permute-start.14 = (bf16[96,1008]{1,0:T(8,128)(2,1)S(1)}, bf16[96,1008]{1,0:T(8,128)(2,1)S(1)}, u32[]{:S(2)}, u32[]{:S(2)}) collective-permute-start(bf16[96,1008]{1,0:T(8,128)(2,1)S(1)} %get-tuple-element.55), channel_id=1, source_target_pairs={{0,14},{2,0},{4,2},{6,4},{8,6},{10,8},{12,10},{14,12},{1,15},{3,1}... | collective-permute-start | bytes 580616 | tf_op jit(solution)/shard_map/ppermute | solution.py:36
  44.0 6.8 %collective-permute-start.17 = (bf16[96,1008]{1,0:T(8,128)(2,1)S(1)}, bf16[96,1008]{1,0:T(8,128)(2,1)S(1)}, u32[]{:S(2)}, u32[]{:S(2)}) collective-permute-start(bf16[96,1008]{1,0:T(8,128)(2,1)S(1)} %get-tuple-element.59), channel_id=1, source_target_pairs={{0,2},{2,4},{4,6},{6,8},{8,10},{10,12},{12,14},{14,0},{1,3},{3,5},... | collective-permute-start | bytes 580616 | tf_op jit(solution)/shard_map/ppermute | solution.py:36
  46.9 8.6 %collective-permute-start.6 = (bf16[96,1008]{1,0:T(8,128)(2,1)S(1)}, bf16[96,1008]{1,0:T(8,128)(2,1)S(1)}, u32[]{:S(2)}, u32[]{:S(2)}) collective-permute-start(bf16[96,1008]{1,0:T(8,128)(2,1)S(1)} %add_convert_fusion.6), channel_id=1, source_target_pairs={{0,2},{2,4},{4,6},{6,8},{8,10},{10,12},{12,14},{14,0},{1,3},{3,5},... | collective-permute-start | bytes 580616 | tf_op jit(solution)/shard_map/ppermute | solution.py:36
  50.8 11.0 %collective-permute-start.18 = (bf16[96,1008]{1,0:T(8,128)(2,1)S(1)}, bf16[96,1008]{1,0:T(8,128)(2,1)S(1)}, u32[]{:S(2)}, u32[]{:S(2)}) collective-permute-start(bf16[96,1008]{1,0:T(8,128)(2,1)S(1)} %add_convert_fusion.2), channel_id=1, source_target_pairs={{0,2},{2,4},{4,6},{6,8},{8,10},{10,12},{12,14},{14,0},{1,3},{3,5},... | collective-permute-start | bytes 580616 | tf_op jit(solution)/shard_map/ppermute | solution.py:36
  55.5 12.4 %collective-permute-start.7 = (bf16[96,1008]{1,0:T(8,128)(2,1)S(1)}, bf16[96,1008]{1,0:T(8,128)(2,1)S(1)}, u32[]{:S(2)}, u32[]{:S(2)}) collective-permute-start(bf16[96,1008]{1,0:T(8,128)(2,1)S(1)} %add_convert_fusion.5), channel_id=1, source_target_pairs={{0,2},{2,4},{4,6},{6,8},{8,10},{10,12},{12,14},{14,0},{1,3},{3,5},... | collective-permute-start | bytes 580616 | tf_op jit(solution)/shard_map/ppermute | solution.py:36
  58.4 9.4 %collective-permute-start.5 = (bf16[96,1008]{1,0:T(8,128)(2,1)S(1)}, bf16[96,1008]{1,0:T(8,128)(2,1)S(1)}, u32[]{:S(2)}, u32[]{:S(2)}) collective-permute-start(bf16[96,1008]{1,0:T(8,128)(2,1)S(1)} %add_convert_fusion.7), channel_id=1, source_target_pairs={{0,14},{2,0},{4,2},{6,4},{8,6},{10,8},{12,10},{14,12},{1,15},{3,1}... | collective-permute-start | bytes 580616 | tf_op jit(solution)/shard_map/ppermute | solution.py:36
  62.3 8.3 %collective-permute-start.16 = (bf16[96,1008]{1,0:T(8,128)(2,1)S(1)}, bf16[96,1008]{1,0:T(8,128)(2,1)S(1)}, u32[]{:S(2)}, u32[]{:S(2)}) collective-permute-start(bf16[96,1008]{1,0:T(8,128)(2,1)S(1)} %add_convert_fusion.3), channel_id=1, source_target_pairs={{0,14},{2,0},{4,2},{6,4},{8,6},{10,8},{12,10},{14,12},{1,15},{3,1}... | collective-permute-start | bytes 580616 | tf_op jit(solution)/shard_map/ppermute | solution.py:36
  68.2 8.1 %collective-permute-start.8 = (bf16[96,1008]{1,0:T(8,128)(2,1)S(1)}, bf16[96,1008]{1,0:T(8,128)(2,1)S(1)}, u32[]{:S(2)}, u32[]{:S(2)}) collective-permute-start(bf16[96,1008]{1,0:T(8,128)(2,1)S(1)} %pad_maximum_fusion.refs_0_.refs_11_), channel_id=1, source_target_pairs={{0,2},{2,4},{4,6},{6,8},{8,10},{10,12},{12,14},{14,0},{1,3},{3,5},... | collective-permute-start | bytes 580616 | tf_op jit(solution)/shard_map/ppermute | solution.py:36
  74.7 6.9 %collective-permute-start.9 = (bf16[96,1008]{1,0:T(8,128)(2,1)S(1)}, bf16[96,1008]{1,0:T(8,128)(2,1)S(1)}, u32[]{:S(2)}, u32[]{:S(2)}) collective-permute-start(bf16[96,1008]{1,0:T(8,128)(2,1)S(1)} %pad_maximum_fusion.refs_0_.refs_11_), channel_id=1, source_target_pairs={{0,14},{2,0},{4,2},{6,4},{8,6},{10,8},{12,10},{14,12},{1,15},{3,1}... | collective-permute-start | bytes 580616 | tf_op jit(solution)/shard_map/ppermute | solution.py:36
  74.8 8.2 %collective-permute-start.21 = (bf16[96,1008]{1,0:T(8,128)(2,1)S(1)}, bf16[96,1008]{1,0:T(8,128)(2,1)S(1)}, u32[]{:S(2)}, u32[]{:S(2)}) collective-permute-start(bf16[96,1008]{1,0:T(8,128)(2,1)S(1)} %pad_maximum_fusion.1.refs_7_.refs_19_), channel_id=1, source_target_pairs={{0,2},{2,4},{4,6},{6,8},{8,10},{10,12},{12,14},{14,0},{1,3},{3,5},... | collective-permute-start | bytes 580616 | tf_op jit(solution)/shard_map/ppermute | solution.py:36
  76.4 9.7 %collective-permute-start.10 = (bf16[96,1008]{1,0:T(8,128)(2,1)S(1)}, bf16[96,1008]{1,0:T(8,128)(2,1)S(1)}, u32[]{:S(2)}, u32[]{:S(2)}) collective-permute-start(bf16[96,1008]{1,0:T(8,128)(2,1)S(1)} %collective-permute-done.8.refs_1_.refs_10_), channel_id=1, source_target_pairs={{0,2},{2,4},{4,6},{6,8},{8,10},{10,12},{12,14},{14,0},{1,3},{3,5},... | collective-permute-start | bytes 580616 | tf_op jit(solution)/shard_map/ppermute | solution.py:36
  81.6 7.2 %collective-permute-start.11 = (bf16[96,1008]{1,0:T(8,128)(2,1)S(1)}, bf16[96,1008]{1,0:T(8,128)(2,1)S(1)}, u32[]{:S(2)}, u32[]{:S(2)}) collective-permute-start(bf16[96,1008]{1,0:T(8,128)(2,1)S(1)} %collective-permute-done.9.refs_2_.refs_9_), channel_id=1, source_target_pairs={{0,14},{2,0},{4,2},{6,4},{8,6},{10,8},{12,10},{14,12},{1,15},{3,1}... | collective-permute-start | bytes 580616 | tf_op jit(solution)/shard_map/ppermute | solution.py:36
  83.0 8.1 %collective-permute-start.23 = (bf16[96,1008]{1,0:T(8,128)(2,1)S(1)}, bf16[96,1008]{1,0:T(8,128)(2,1)S(1)}, u32[]{:S(2)}, u32[]{:S(2)}) collective-permute-start(bf16[96,1008]{1,0:T(8,128)(2,1)S(1)} %collective-permute-done.21.refs_8_.refs_18_), channel_id=1, source_target_pairs={{0,2},{2,4},{4,6},{6,8},{8,10},{10,12},{12,14},{14,0},{1,3},{3,5},... | collective-permute-start | bytes 580616 | tf_op jit(solution)/shard_map/ppermute | solution.py:36
  86.1 8.9 %collective-permute-start.12 = (bf16[96,1008]{1,0:T(8,128)(2,1)S(1)}, bf16[96,1008]{1,0:T(8,128)(2,1)S(1)}, u32[]{:S(2)}, u32[]{:S(2)}) collective-permute-start(bf16[96,1008]{1,0:T(8,128)(2,1)S(1)} %collective-permute-done.10.refs_3_.refs_8_), channel_id=1, source_target_pairs={{0,2},{2,4},{4,6},{6,8},{8,10},{10,12},{12,14},{14,0},{1,3},{3,5},... | collective-permute-start | bytes 580616 | tf_op jit(solution)/shard_map/ppermute | solution.py:36
  86.1 8.9 %collective-permute-start.26 = (bf16[96,1008]{1,0:T(8,128)(2,1)S(1)}, bf16[96,1008]{1,0:T(8,128)(2,1)S(1)}, u32[]{:S(2)}, u32[]{:S(2)}) collective-permute-start(bf16[96,1008]{1,0:T(8,128)(2,1)S(1)} %collective-permute-done.24.refs_11_.refs_15_), channel_id=1, source_target_pairs={{0,14},{2,0},{4,2},{6,4},{8,6},{10,8},{12,10},{14,12},{1,15},{3,1}... | collective-permute-start | bytes 580616 | tf_op jit(solution)/shard_map/ppermute | solution.py:36
  88.8 8.9 %collective-permute-start.13 = (bf16[96,1008]{1,0:T(8,128)(2,1)S(1)}, bf16[96,1008]{1,0:T(8,128)(2,1)S(1)}, u32[]{:S(2)}, u32[]{:S(2)}) collective-permute-start(bf16[96,1008]{1,0:T(8,128)(2,1)S(1)} %collective-permute-done.11.refs_4_.refs_7_), channel_id=1, source_target_pairs={{0,14},{2,0},{4,2},{6,4},{8,6},{10,8},{12,10},{14,12},{1,15},{3,1}... | collective-permute-start | bytes 580616 | tf_op jit(solution)/shard_map/ppermute | solution.py:36
  95.0 8.1 %collective-permute-start.27 = (bf16[96,1008]{1,0:T(8,128)(2,1)S(1)}, bf16[96,1008]{1,0:T(8,128)(2,1)S(1)}, u32[]{:S(2)}, u32[]{:S(2)}) collective-permute-start(bf16[96,1008]{1,0:T(8,128)(2,1)S(1)} %collective-permute-done.12.refs_5_.refs_6_), channel_id=1, source_target_pairs={{0,2},{2,4},{4,6},{6,8},{8,10},{10,12},{12,14},{14,0},{1,3},{3,5},... | collective-permute-start | bytes 580616 | tf_op jit(solution)/shard_map/ppermute | solution.py:36
  95.0 8.1 %collective-permute-start.28 = (bf16[96,1008]{1,0:T(8,128)(2,1)S(1)}, bf16[96,1008]{1,0:T(8,128)(2,1)S(1)}, u32[]{:S(2)}, u32[]{:S(2)}) collective-permute-start(bf16[96,1008]{1,0:T(8,128)(2,1)S(1)} %collective-permute-done.26.refs_13_), channel_id=1, source_target_pairs={{0,14},{2,0},{4,2},{6,4},{8,6},{10,8},{12,10},{14,12},{1,15},{3,1}... | collective-permute-start | bytes 580616 | tf_op jit(solution)/shard_map/ppermute | solution.py:36
  104.1 11.3 %collective-permute-start.29 = (bf16[672,768]{1,0:T(8,128)(2,1)S(1)}, bf16[672,768]{1,0:T(8,128)(2,1)S(1)}, u32[]{:S(2)}, u32[]{:S(2)}) collective-permute-start(bf16[672,768]{1,0:T(8,128)(2,1)S(1)} %get-tuple-element.63), channel_id=1, source_target_pairs={{0,16},{16,0},{1,17},{17,1},{2,18},{18,2},{3,19},{19,3},{4,20},{20... | collective-permute-start | bytes 3096584 | tf_op jit(solution)/shard_map/ppermute | solution.py:28
  117.2 27.2 %all-to-all-start.1 = ((bf16[8,96,768]{2,1,0:T(8,128)(2,1)}), bf16[8,96,768]{2,1,0:T(8,128)(2,1)S(1)}, u32[]{:S(2)}, u32[]{:S(2)}) async-start(bf16[8,96,768]{2,1,0:T(8,128)(2,1)} %pair_sum.1), calls=%async_computation.1 | async-start | bytes 2359296 | tf_op jit(solution)/shard_map/all_to_all | solution.py:32
  120.8 22.4 %collective-permute-start.31 = (bf16[192,1008]{1,0:T(8,128)(2,1)S(1)}, bf16[192,1008]{1,0:T(8,128)(2,1)S(1)}, u32[]{:S(2)}, u32[]{:S(2)}) collective-permute-start(bf16[192,1008]{1,0:T(8,128)(2,1)S(1)} %get-tuple-element.76), channel_id=1, source_target_pairs={{0,1},{1,0},{2,3},{3,2},{4,5},{5,4},{6,7},{7,6},{8,9},{9,8},{10,11... | collective-permute-start | bytes 1161224 | tf_op jit(solution)/shard_map/ppermute | solution.py:284
  (18 other events, 138.7 us)
